TPU v7x, 256 devices: a whole 4x4x8 slice. The times are simulated.
256 devices in a mesh: leaf: 256 (over y, x, z, core).
Axes of the slice: x: 4, y: 4, z: 8, core: 2. Of those that a mesh axis runs over, the one named last changes fastest.
Arguments:
- points: float32 [32, 262144], P(None, 'leaf'), may hold values from -6 to 6
- charges: float32 [32, 262144], P(None, 'leaf'), may hold values from -6 to 6
- leaf_skeleton: int32 [256, 256], P('leaf'), may hold values from 0 to 1023, as said below
- upper_skeleton: int32 [256, 3, 256], P('leaf'), may hold values from 0 to 511, as said below
- leaf_projection: float32 [256, 256, 1024], P('leaf'), as said below
- upper_projection: float32 [256, 3, 256, 512], P('leaf'), as said below
- near_leaves: int32 [256, 7], P('leaf'), may hold values from 0 to 255, as said below
- far_codes: int32 [256, 4, 2], P('leaf'), may hold values from 1 to 3, as said below
- regularizer: float32 [32], replicated, may hold values from 0.5 to 2
Outputs:
- potential: float32 [32, 262144], P(None, 'leaf')
Inputs may be any that keep to these rules, and one draw needn't show every extreme that they name: `leaf_skeleton`: each row holds 256 distinct increasing indices of points within its leaf. `upper_skeleton`: entry [i, k] holds 256 distinct increasing indices into the 512 candidate skeleton points of the level k+1 node that holds leaf i, and is equal for all leaves of that node. `leaf_projection`: row r of leaf i's matrix is 1 in column leaf_skeleton[i, r] and 0 in the other skeleton columns. `upper_projection`: row r of entry [i, k] is 1 in column upper_skeleton[i, k, r] and 0 in the other skeleton columns; the entry is equal for all leaves of the level k+1 node that holds leaf i. `near_leaves`: row i holds 7 distinct leaves: i itself first, then leaves within 6 of i. `far_codes`: entry [i, k] holds two distinct increasing codes for the level k node that holds leaf i, equal for all leaves of that node.
All inputs are finite; a program needn't handle non-finite values.
Results may differ from a plain program's by a relative error of at most 0.0003.
Values sent between devices are 32-bit elements; how exact they have to be, the bound alone decides.
No kernel may reach another device: no remote copies, remote signals or barrier semaphores. Data moves between devices by JAX's collectives and lax.ppermute only.
A program may use at most 64 MiB of HBM per device.

v0:
```python
import jax
import jax.numpy as jnp
from jax import lax
from jax.sharding import PartitionSpec as P

RANK = 256
LEVELS = 4
NEAR_SPAN = 6
FAR = 2


inverse_width = 1.0 / 16.0


def shifted(value, axis, steps):
    count = lax.axis_size(axis)
    leading, last = (max(0, -steps), min(count, count - steps))
    return lax.ppermute(value, axis, [(source, source + steps) for source in range(leading, last)])


def partner(value, axis, bit):
    mask = 2**bit
    pairs = [(source, source ^ mask) for source in range(lax.axis_size(axis))]
    return lax.ppermute(value, axis, pairs)


def kernel(left_set, right_set):
    cross = lax.dot_general(
        left_set,
        right_set,
        (((0,), (0,)), ((), ())),
        precision=lax.Precision.HIGHEST,
        preferred_element_type=jnp.float32,
    )
    distance = (
        jnp.sum(left_set * left_set, axis=0)[:, None]
        + jnp.sum(right_set * right_set, axis=0)[None, :]
        - 2.0 * cross
    )
    return jnp.exp(-inverse_width * distance)


def apply_rows(weights, kernel_tile):
    return lax.dot_general(
        weights,
        kernel_tile,
        (((1,), (1,)), ((), ())),
        precision=lax.Precision.HIGHEST,
        preferred_element_type=jnp.float32,
    )


def spread(weights, kernel_tile):
    return jnp.dot(
        weights, kernel_tile, precision=lax.Precision.HIGHEST, preferred_element_type=jnp.float32
    )


def far_field(node_data, sibling, cousin_pair, codes):
    stacked_points = jnp.stack([sibling[0], cousin_pair[0], cousin_pair[2]])
    stacked_weights = jnp.stack([sibling[1], cousin_pair[1], cousin_pair[3]])
    accum = jnp.zeros(node_data[1].shape, jnp.float32)
    for position in range(FAR):
        chosen_slot = codes[position] - 1
        accum = accum + apply_rows(
            stacked_weights[chosen_slot], kernel(node_data[0], stacked_points[chosen_slot])
        )
    return accum


def merge_children(node_data, sibling, chosen, projection, is_right):
    cand_points = jnp.where(
        is_right == 1,
        jnp.concatenate([sibling[0], node_data[0]], axis=1),
        jnp.concatenate([node_data[0], sibling[0]], axis=1),
    )
    cand_weights = jnp.where(
        is_right == 1,
        jnp.concatenate([sibling[1], node_data[1]], axis=1),
        jnp.concatenate([node_data[1], sibling[1]], axis=1),
    )
    parent_points = jnp.take(cand_points, chosen, axis=1)
    parent_weights = apply_rows(cand_weights, projection)
    return (parent_points, parent_weights)


def body(
    points,
    charges,
    leaf_skeleton,
    upper_skeleton,
    leaf_projection,
    upper_projection,
    near_leaves,
    far_codes,
    regularizer,
):
    device = lax.axis_index("leaf")
    leaf_size = points.shape[1]
    fetched = {}
    for offset in range(-NEAR_SPAN, NEAR_SPAN + 1):
        if offset != 0:
            fetched[offset] = shifted((points, charges), "leaf", -offset)
    fetched[0] = (points, charges)
    stacked_points = jnp.stack([fetched[offset][0] for offset in range(-NEAR_SPAN, NEAR_SPAN + 1)])
    stacked_charges = jnp.stack([fetched[offset][1] for offset in range(-NEAR_SPAN, NEAR_SPAN + 1)])
    block_rows = min(128, leaf_size)
    block_count = leaf_size // block_rows
    own_blocks = points.reshape(points.shape[0], block_count, block_rows).transpose(1, 0, 2)

    def near_block(own_part):
        accum = jnp.zeros((charges.shape[0], block_rows), jnp.float32)
        for position in range(near_leaves.shape[1]):
            chosen_slot = near_leaves[0, position] - device + NEAR_SPAN
            accum = accum + apply_rows(
                stacked_charges[chosen_slot], kernel(own_part, stacked_points[chosen_slot])
            )
        return accum

    near_field = (
        lax.map(near_block, own_blocks).transpose(1, 0, 2).reshape(charges.shape[0], leaf_size)
    )
    leaf_points = jnp.take(points, leaf_skeleton[0], axis=1)
    leaf_matrix = leaf_projection[0]
    node_data = (leaf_points, apply_rows(charges, leaf_matrix))
    far_list = []
    tiles = []
    for height in range(LEVELS):
        sibling = partner((node_data[0], node_data[1]), "leaf", height)
        cousin_pair = partner(
            (node_data[0], node_data[1], sibling[0], sibling[1]), "leaf", height + 1
        )
        far_list.append(far_field(node_data, sibling, cousin_pair, far_codes[0, height]))
        if height + 1 < LEVELS:
            is_right = jnp.bitwise_and(jnp.right_shift(device, height), 1)
            projection = upper_projection[0, height]
            node_data = merge_children(
                node_data, sibling, upper_skeleton[0, height], projection, is_right
            )
            tiles.append(projection)
    local_field = far_list[LEVELS - 1]
    for height in reversed(range(LEVELS - 1)):
        down_field = spread(local_field, tiles[height])
        is_right = jnp.bitwise_and(jnp.right_shift(device, height), 1)
        half_field = lax.dynamic_slice_in_dim(down_field, is_right * RANK, RANK, axis=1)
        local_field = far_list[height] + half_field
    far_out = spread(local_field, leaf_matrix)
    return far_out + near_field + regularizer[:, None] * charges


def solution(mesh):
    placed = (
        P(None, "leaf"),
        P(None, "leaf"),
        P("leaf", None),
        P("leaf", None, None),
        P("leaf", None, None),
        P("leaf", None, None, None),
        P("leaf", None),
        P("leaf", None, None),
        P(),
    )
    return jax.shard_map(
        body, mesh=mesh, in_specs=placed, out_specs=P(None, "leaf"), check_vma=False
    )
```

profile of v0, /device:TPU:100, one launch (start us, length us, event | category | flops | bytes accessed | tf_op | source)
XLA Modules:
  0.0 382.0 jit_solution(9972308029712651342)
XLA Ops:
  0.0 6.1 %collective-permute-start.24 = (f32[32,1024]{1,0:T(8,128)}, f32[32,1024]{1,0:T(8,128)}, u32[]{:S(2)}, u32[]{:S(2)}) collective-permute-start(f32[32,1024]{1,0:T(8,128)} %param.13), channel_id=1, source_target_pairs={{0,6},{1,7},{2,8},{3,9},{4,10},{5,11},{6,12},{7,13},{8,14},{9,15},... | collective-permute-start | bytes 393224 | tf_op jit(solution)/shard_map/ppermute | solution.py:18
  6.1 1.9 collective-permute-start.25
  8.0 2.8 collective-permute-start.26
  14.8 2.0 collective-permute-start.3
  21.5 1.9 fusion.67
  54.7 2.8 collective-permute-done.6
  60.4 2.3 collective-permute-start.7
  65.2 2.6 collective-permute-start.27
  67.8 1.9 collective-permute-start.15
  70.7 5.4 %collective-permute-done.15 = f32[32,256]{1,0:T(8,128)} collective-permute-done((f32[32,256]{1,0:T(8,128)}, f32[32,256]{1,0:T(8,128)}, u32[]{:S(2)}, u32[]{:S(2)}) %collective-permute-start.15) | collective-permute-done | bytes 32800 | tf_op jit(solution)/shard_map/ppermute | solution.py:24
  77.8 3.5 collective-permute-done.12
  81.4 2.3 collective-permute-start.28
  83.7 2.0 fusion.71
  87.0 2.0 collective-permute-start.29
  90.0 3.6 collective-permute-start.30
  94.5 3.5 collective-permute-start.31
  98.0 1.9 collective-permute-start.32
  100.0 6.2 %collective-permute-start.33 = (f32[32,1024]{1,0:T(8,128)S(1)}, f32[32,1024]{1,0:T(8,128)S(1)}, u32[]{:S(2)}, u32[]{:S(2)}) collective-permute-start(f32[32,1024]{1,0:T(8,128)S(1)} %copy-done.8), channel_id=1, source_target_pairs={{4,0},{5,1},{6,2},{7,3},{8,4},{9,5},{10,6},{11,7},{12,8},{13,9},{1... | collective-permute-start | bytes 393224 | tf_op jit(solution)/shard_map/ppermute | solution.py:18
  106.2 2.5 collective-permute-start.36
  108.8 8.4 %collective-permute-done.36 = f32[32,1024]{1,0:T(8,128)S(1)} collective-permute-done((f32[32,1024]{1,0:T(8,128)}, f32[32,1024]{1,0:T(8,128)S(1)}, u32[]{:S(2)}, u32[]{:S(2)}) %collective-permute-start.36) | collective-permute-done | bytes 131104 | tf_op jit(solution)/shard_map/ppermute | solution.py:18
  117.2 7.9 %collective-permute-start.37 = (f32[32,1024]{1,0:T(8,128)}, f32[32,1024]{1,0:T(8,128)S(1)}, u32[]{:S(2)}, u32[]{:S(2)}) collective-permute-start(f32[32,1024]{1,0:T(8,128)} %param.14), channel_id=1, source_target_pairs={{0,5},{1,6},{2,7},{3,8},{4,9},{5,10},{6,11},{7,12},{8,13},{9,14},{... | collective-permute-start | bytes 393224 | tf_op jit(solution)/shard_map/ppermute | solution.py:18
  125.2 7.0 %collective-permute-done.37 = f32[32,1024]{1,0:T(8,128)S(1)} collective-permute-done((f32[32,1024]{1,0:T(8,128)}, f32[32,1024]{1,0:T(8,128)S(1)}, u32[]{:S(2)}, u32[]{:S(2)}) %collective-permute-start.37) | collective-permute-done | bytes 131104 | tf_op jit(solution)/shard_map/ppermute | solution.py:18
  132.2 5.7 %collective-permute-start.38 = (f32[32,1024]{1,0:T(8,128)}, f32[32,1024]{1,0:T(8,128)S(1)}, u32[]{:S(2)}, u32[]{:S(2)}) collective-permute-start(f32[32,1024]{1,0:T(8,128)} %param.14), channel_id=1, source_target_pairs={{0,4},{1,5},{2,6},{3,7},{4,8},{5,9},{6,10},{7,11},{8,12},{9,13},{1... | collective-permute-start | bytes 393224 | tf_op jit(solution)/shard_map/ppermute | solution.py:18
  137.9 6.1 %collective-permute-done.38 = f32[32,1024]{1,0:T(8,128)S(1)} collective-permute-done((f32[32,1024]{1,0:T(8,128)}, f32[32,1024]{1,0:T(8,128)S(1)}, u32[]{:S(2)}, u32[]{:S(2)}) %collective-permute-start.38) | collective-permute-done | bytes 131104 | tf_op jit(solution)/shard_map/ppermute | solution.py:18
  145.9 5.7 %collective-permute-done.39 = f32[32,1024]{1,0:T(8,128)S(1)} collective-permute-done((f32[32,1024]{1,0:T(8,128)}, f32[32,1024]{1,0:T(8,128)S(1)}, u32[]{:S(2)}, u32[]{:S(2)}) %collective-permute-start.39) | collective-permute-done | bytes 131104 | tf_op jit(solution)/shard_map/ppermute | solution.py:18
  151.7 6.9 %collective-permute-start.40 = (f32[32,1024]{1,0:T(8,128)}, f32[32,1024]{1,0:T(8,128)S(1)}, u32[]{:S(2)}, u32[]{:S(2)}) collective-permute-start(f32[32,1024]{1,0:T(8,128)} %param.14), channel_id=1, source_target_pairs={{0,2},{1,3},{2,4},{3,5},{4,6},{5,7},{6,8},{7,9},{8,10},{9,11},{10,... | collective-permute-start | bytes 393224 | tf_op jit(solution)/shard_map/ppermute | solution.py:18
  158.6 2.8 collective-permute-done.40
  163.3 4.5 %collective-permute-done.41 = f32[32,1024]{1,0:T(8,128)S(1)} collective-permute-done((f32[32,1024]{1,0:T(8,128)}, f32[32,1024]{1,0:T(8,128)S(1)}, u32[]{:S(2)}, u32[]{:S(2)}) %collective-permute-start.41) | collective-permute-done | bytes 131104 | tf_op jit(solution)/shard_map/ppermute | solution.py:18
  167.9 5.2 %collective-permute-start.34 = (f32[32,1024]{1,0:T(8,128)S(1)}, f32[32,1024]{1,0:T(8,128)S(1)}, u32[]{:S(2)}, u32[]{:S(2)}) collective-permute-start(f32[32,1024]{1,0:T(8,128)S(1)} %copy-done.8), channel_id=1, source_target_pairs={{5,0},{6,1},{7,2},{8,3},{9,4},{10,5},{11,6},{12,7},{13,8},{14,9},{... | collective-permute-start | bytes 393224 | tf_op jit(solution)/shard_map/ppermute | solution.py:18
  174.0 7.0 %collective-permute-start.35 = (f32[32,1024]{1,0:T(8,128)S(1)}, f32[32,1024]{1,0:T(8,128)S(1)}, u32[]{:S(2)}, u32[]{:S(2)}) collective-permute-start(f32[32,1024]{1,0:T(8,128)S(1)} %copy-done.8), channel_id=1, source_target_pairs={{6,0},{7,1},{8,2},{9,3},{10,4},{11,5},{12,6},{13,7},{14,8},{15,9},... | collective-permute-start | bytes 393224 | tf_op jit(solution)/shard_map/ppermute | solution.py:18
  181.0 2.2 collective-permute-start.42
  183.3 1.9 collective-permute-start.43
  185.2 2.0 collective-permute-start.44
  187.3 3.0 collective-permute-start.45
  190.3 7.3 %collective-permute-start.46 = (f32[32,1024]{1,0:T(8,128)}, f32[32,1024]{1,0:T(8,128)S(1)}, u32[]{:S(2)}, u32[]{:S(2)}) collective-permute-start(f32[32,1024]{1,0:T(8,128)} %param.14), channel_id=1, source_target_pairs={{5,0},{6,1},{7,2},{8,3},{9,4},{10,5},{11,6},{12,7},{13,8},{14,9},{... | collective-permute-start | bytes 393224 | tf_op jit(solution)/shard_map/ppermute | solution.py:18
  197.7 2.2 collective-permute-start.47
  199.9 6.7 %collective-permute-start.16 = (f32[32,256]{1,0:T(8,128)}, f32[32,256]{1,0:T(8,128)}, u32[]{:S(2)}, u32[]{:S(2)}) collective-permute-start(f32[32,256]{1,0:T(8,128)} %get-tuple-element.496), channel_id=1, source_target_pairs={{0,8},{1,9},{2,10},{3,11},{4,12},{5,13},{6,14},{7,15},{8,0},{9,1},... | collective-permute-start | bytes 98312 | tf_op jit(solution)/shard_map/ppermute | solution.py:24
  206.7 3.7 collective-permute-done.45
  210.4 2.3 collective-permute-start.21
  212.8 2.5 collective-permute-done.46
  215.3 5.9 %collective-permute-start.22 = (f32[32,256]{0,1:T(8,128)}, f32[32,256]{0,1:T(8,128)}, u32[]{:S(2)}, u32[]{:S(2)}) collective-permute-start(f32[32,256]{0,1:T(8,128)} %get-tuple-element.494), channel_id=1, source_target_pairs={{0,16},{1,17},{2,18},{3,19},{4,20},{5,21},{6,22},{7,23},{8,24},{9,... | collective-permute-start | bytes 98312 | tf_op jit(solution)/shard_map/ppermute | solution.py:24
  222.0 7.0 %collective-permute-done.47 = f32[32,1024]{1,0:T(8,128)S(1)} collective-permute-done((f32[32,1024]{1,0:T(8,128)}, f32[32,1024]{1,0:T(8,128)S(1)}, u32[]{:S(2)}, u32[]{:S(2)}) %collective-permute-start.47) | collective-permute-done | bytes 131104 | tf_op jit(solution)/shard_map/ppermute | solution.py:18
  229.0 8.5 %collective-permute-start.17 = (f32[32,256]{1,0:T(8,128)}, f32[32,256]{1,0:T(8,128)}, u32[]{:S(2)}, u32[]{:S(2)}) collective-permute-start(f32[32,256]{1,0:T(8,128)} %collective-permute-done.15), channel_id=1, source_target_pairs={{0,8},{1,9},{2,10},{3,11},{4,12},{5,13},{6,14},{7,15},{8,0},{9,1},... | collective-permute-start | bytes 98312 | tf_op jit(solution)/shard_map/ppermute | solution.py:24
  238.6 105.7 %while.13 = (s32[]{:T(128)}, f32[8,32,128]{2,1,0:T(8,128)}, f32[8,32,128]{2,0,1:T(8,128)}, f32[1024]{0:T(1024)}, f32[1,32,1024]{2,1,0:T(8,128)S(1)}, /*index=5*/...) while((s32[]{:T(128)}, f32[8,32,128]{2,1,0:T(8,128)}, ...), condition=%wide.region_21.23_spmd, body=%wide.region_19.22_spmd.sunk | while | flops 708345728 | bytes 12747685 | solution.py:121
  344.3 5.9 %collective-permute-start.14 = (f32[32,256]{1,0:T(8,128)}, f32[32,256]{1,0:T(8,128)S(1)}, u32[]{:S(2)}, u32[]{:S(2)}) collective-permute-start(f32[32,256]{1,0:T(8,128)} %copy-done.16), channel_id=1, source_target_pairs={{0,8},{1,9},{2,10},{3,11},{4,12},{5,13},{6,14},{7,15},{8,0},{9,1},... | collective-permute-start | bytes 98312 | tf_op jit(solution)/shard_map/ppermute | solution.py:24
  353.5 12.7 %collective-permute-start.19 = (f32[32,256]{1,0:T(8,128)}, f32[32,256]{1,0:T(8,128)S(1)}, u32[]{:S(2)}, u32[]{:S(2)}) collective-permute-start(f32[32,256]{1,0:T(8,128)} %fusion.71), channel_id=1, source_target_pairs={{0,16},{1,17},{2,18},{3,19},{4,20},{5,21},{6,22},{7,23},{8,24},{9,... | collective-permute-start | bytes 98312 | tf_op jit(solution)/shard_map/ppermute | solution.py:24
  369.4 2.4 collective-permute-start.20
  379.6 2.3 fusion.62
  (418 shorter events, 161.4 us)
Async XLA Ops:
  0.0 87.0 %collective-permute-start.24 = (f32[32,1024]{1,0:T(8,128)}, f32[32,1024]{1,0:T(8,128)}, u32[]{:S(2)}, u32[]{:S(2)}) collective-permute-start(f32[32,1024]{1,0:T(8,128)} %param.13), channel_id=1, source_target_pairs={{0,6},{1,7},{2,8},{3,9},{4,10},{5,11},{6,12},{7,13},{8,14},{9,15},... | collective-permute-start | bytes 393224 | tf_op jit(solution)/shard_map/ppermute | solution.py:18
  6.1 83.9 %collective-permute-start.25 = (f32[32,1024]{1,0:T(8,128)}, f32[32,1024]{1,0:T(8,128)}, u32[]{:S(2)}, u32[]{:S(2)}) collective-permute-start(f32[32,1024]{1,0:T(8,128)} %param.13), channel_id=1, source_target_pairs={{0,5},{1,6},{2,7},{3,8},{4,9},{5,10},{6,11},{7,12},{8,13},{9,14},{... | collective-permute-start | bytes 393224 | tf_op jit(solution)/shard_map/ppermute | solution.py:18
  8.0 86.5 %collective-permute-start.26 = (f32[32,1024]{1,0:T(8,128)}, f32[32,1024]{1,0:T(8,128)S(1)}, u32[]{:S(2)}, u32[]{:S(2)}) collective-permute-start(f32[32,1024]{1,0:T(8,128)} %param.13), channel_id=1, source_target_pairs={{0,4},{1,5},{2,6},{3,7},{4,8},{5,9},{6,10},{7,11},{8,12},{9,13},{1... | collective-permute-start | bytes 393224 | tf_op jit(solution)/shard_map/ppermute | solution.py:18
  14.8 24.0 %collective-permute-start.3 = (f32[32,256]{1,0:T(8,128)S(1)}, f32[32,256]{1,0:T(8,128)S(1)}, u32[]{:S(2)}, u32[]{:S(2)}) collective-permute-start(f32[32,256]{1,0:T(8,128)S(1)} %get-tuple-element.500), channel_id=1, source_target_pairs={{0,1},{1,0},{2,3},{3,2},{4,5},{5,4},{6,7},{7,6},{8,9},{9,8},{10,11... | collective-permute-start | bytes 98312 | tf_op jit(solution)/shard_map/ppermute | solution.py:24
  16.9 26.9 %collective-permute-start.4 = (f32[32,256]{1,0:T(8,128)S(1)}, f32[32,256]{1,0:T(8,128)}, u32[]{:S(2)}, u32[]{:S(2)}) collective-permute-start(f32[32,256]{1,0:T(8,128)S(1)} %get-tuple-element.500), channel_id=1, source_target_pairs={{0,2},{1,3},{2,0},{3,1},{4,6},{5,7},{6,4},{7,5},{8,10},{9,11},{10,... | collective-permute-start | bytes 98312 | tf_op jit(solution)/shard_map/ppermute | solution.py:24
  38.8 1.2 collective-permute-start
  40.1 3.9 %collective-permute-start.5 = (f32[32,256]{1,0:T(8,128)S(1)}, f32[32,256]{1,0:T(8,128)S(1)}, u32[]{:S(2)}, u32[]{:S(2)}) collective-permute-start(f32[32,256]{1,0:T(8,128)S(1)} %collective-permute-done.3), channel_id=1, source_target_pairs={{0,2},{1,3},{2,0},{3,1},{4,6},{5,7},{6,4},{7,5},{8,10},{9,11},{10,... | collective-permute-start | bytes 98312 | tf_op jit(solution)/shard_map/ppermute | solution.py:24
  43.8 5.9 %collective-permute-start.1 = (f32[32,256]{1,0:T(8,128)S(1)}, f32[32,256]{1,0:T(8,128)S(1)}, u32[]{:S(2)}, u32[]{:S(2)}) collective-permute-start(f32[32,256]{1,0:T(8,128)S(1)} %fusion.67), channel_id=1, source_target_pairs={{0,2},{1,3},{2,0},{3,1},{4,6},{5,7},{6,4},{7,5},{8,10},{9,11},{10,... | collective-permute-start | bytes 98312 | tf_op jit(solution)/shard_map/ppermute | solution.py:24
  44.0 5.8 %collective-permute-start.2 = (f32[32,256]{1,0:T(8,128)S(1)}, f32[32,256]{1,0:T(8,128)S(1)}, u32[]{:S(2)}, u32[]{:S(2)}) collective-permute-start(f32[32,256]{1,0:T(8,128)S(1)} %collective-permute-done), channel_id=1, source_target_pairs={{0,2},{1,3},{2,0},{3,1},{4,6},{5,7},{6,4},{7,5},{8,10},{9,11},{10,... | collective-permute-start | bytes 98312 | tf_op jit(solution)/shard_map/ppermute | solution.py:24
  49.7 3.9 %collective-permute-start.9 = (f32[32,256]{1,0:T(8,128)S(1)}, f32[32,256]{1,0:T(8,128)S(1)}, u32[]{:S(2)}, u32[]{:S(2)}) collective-permute-start(f32[32,256]{1,0:T(8,128)S(1)} %get-tuple-element.498), channel_id=1, source_target_pairs={{0,2},{1,3},{2,0},{3,1},{4,6},{5,7},{6,4},{7,5},{8,10},{9,11},{10,... | collective-permute-start | bytes 98312 | tf_op jit(solution)/shard_map/ppermute | solution.py:24
  49.8 10.6 %collective-permute-start.10 = (f32[32,256]{1,0:T(8,128)S(1)}, f32[32,256]{1,0:T(8,128)S(1)}, u32[]{:S(2)}, u32[]{:S(2)}) collective-permute-start(f32[32,256]{1,0:T(8,128)S(1)} %get-tuple-element.498), channel_id=1, source_target_pairs={{0,4},{1,5},{2,6},{3,7},{4,0},{5,1},{6,2},{7,3},{8,12},{9,13},{10,... | collective-permute-start | bytes 98312 | tf_op jit(solution)/shard_map/ppermute | solution.py:24
  53.6 3.9 %collective-permute-start.6 = (f32[32,256]{1,0:T(8,128)S(1)}, f32[32,256]{1,0:T(8,128)S(1)}, u32[]{:S(2)}, u32[]{:S(2)}) collective-permute-start(f32[32,256]{1,0:T(8,128)S(1)} %fusion.79), channel_id=1, source_target_pairs={{0,2},{1,3},{2,0},{3,1},{4,6},{5,7},{6,4},{7,5},{8,10},{9,11},{10,... | collective-permute-start | bytes 98312 | tf_op jit(solution)/shard_map/ppermute | solution.py:24
  57.5 5.3 %collective-permute-start.11 = (f32[32,256]{1,0:T(8,128)S(1)}, f32[32,256]{1,0:T(8,128)S(1)}, u32[]{:S(2)}, u32[]{:S(2)}) collective-permute-start(f32[32,256]{1,0:T(8,128)S(1)} %collective-permute-done.9), channel_id=1, source_target_pairs={{0,4},{1,5},{2,6},{3,7},{4,0},{5,1},{6,2},{7,3},{8,12},{9,13},{10,... | collective-permute-start | bytes 98312 | tf_op jit(solution)/shard_map/ppermute | solution.py:24
  60.4 4.8 %collective-permute-start.7 = (f32[32,256]{1,0:T(8,128)S(1)}, f32[32,256]{1,0:T(8,128)S(1)}, u32[]{:S(2)}, u32[]{:S(2)}) collective-permute-start(f32[32,256]{1,0:T(8,128)S(1)} %fusion.79), channel_id=1, source_target_pairs={{0,4},{1,5},{2,6},{3,7},{4,0},{5,1},{6,2},{7,3},{8,12},{9,13},{10,... | collective-permute-start | bytes 98312 | tf_op jit(solution)/shard_map/ppermute | solution.py:24
  62.7 5.1 %collective-permute-start.8 = (f32[32,256]{1,0:T(8,128)S(1)}, f32[32,256]{1,0:T(8,128)S(1)}, u32[]{:S(2)}, u32[]{:S(2)}) collective-permute-start(f32[32,256]{1,0:T(8,128)S(1)} %collective-permute-done.6), channel_id=1, source_target_pairs={{0,4},{1,5},{2,6},{3,7},{4,0},{5,1},{6,2},{7,3},{8,12},{9,13},{10,... | collective-permute-start | bytes 98312 | tf_op jit(solution)/shard_map/ppermute | solution.py:24
  65.2 32.8 %collective-permute-start.27 = (f32[32,1024]{1,0:T(8,128)S(1)}, f32[32,1024]{1,0:T(8,128)S(1)}, u32[]{:S(2)}, u32[]{:S(2)}) collective-permute-start(f32[32,1024]{1,0:T(8,128)S(1)} %copy-done.8), channel_id=1, source_target_pairs={{0,3},{1,4},{2,5},{3,6},{4,7},{5,8},{6,9},{7,10},{8,11},{9,12},{10... | collective-permute-start | bytes 393224 | tf_op jit(solution)/shard_map/ppermute | solution.py:18
  67.8 8.3 %collective-permute-start.15 = (f32[32,256]{1,0:T(8,128)}, f32[32,256]{1,0:T(8,128)}, u32[]{:S(2)}, u32[]{:S(2)}) collective-permute-start(f32[32,256]{1,0:T(8,128)} %get-tuple-element.496), channel_id=1, source_target_pairs={{0,4},{1,5},{2,6},{3,7},{4,0},{5,1},{6,2},{7,3},{8,12},{9,13},{10,... | collective-permute-start | bytes 98312 | tf_op jit(solution)/shard_map/ppermute | solution.py:24
  76.1 5.3 %collective-permute-start.12 = (f32[32,256]{1,0:T(8,128)}, f32[32,256]{1,0:T(8,128)S(1)}, u32[]{:S(2)}, u32[]{:S(2)}) collective-permute-start(f32[32,256]{1,0:T(8,128)} %fusion.75), channel_id=1, source_target_pairs={{0,4},{1,5},{2,6},{3,7},{4,0},{5,1},{6,2},{7,3},{8,12},{9,13},{10,... | collective-permute-start | bytes 98312 | tf_op jit(solution)/shard_map/ppermute | solution.py:24
  81.4 18.6 %collective-permute-start.28 = (f32[32,1024]{1,0:T(8,128)S(1)}, f32[32,1024]{1,0:T(8,128)S(1)}, u32[]{:S(2)}, u32[]{:S(2)}) collective-permute-start(f32[32,1024]{1,0:T(8,128)S(1)} %copy-done.8), channel_id=1, source_target_pairs={{0,2},{1,3},{2,4},{3,5},{4,6},{5,7},{6,8},{7,9},{8,10},{9,11},{10,... | collective-permute-start | bytes 393224 | tf_op jit(solution)/shard_map/ppermute | solution.py:18
  87.0 19.2 %collective-permute-start.29 = (f32[32,1024]{1,0:T(8,128)S(1)}, f32[32,1024]{1,0:T(8,128)S(1)}, u32[]{:S(2)}, u32[]{:S(2)}) collective-permute-start(f32[32,1024]{1,0:T(8,128)S(1)} %copy-done.8), channel_id=1, source_target_pairs={{0,1},{1,2},{2,3},{3,4},{4,5},{5,6},{6,7},{7,8},{8,9},{9,10},{10,1... | collective-permute-start | bytes 393224 | tf_op jit(solution)/shard_map/ppermute | solution.py:18
  90.0 84.0 %collective-permute-start.30 = (f32[32,1024]{1,0:T(8,128)S(1)}, f32[32,1024]{1,0:T(8,128)S(1)}, u32[]{:S(2)}, u32[]{:S(2)}) collective-permute-start(f32[32,1024]{1,0:T(8,128)S(1)} %copy-done.8), channel_id=1, source_target_pairs={{1,0},{2,1},{3,2},{4,3},{5,4},{6,5},{7,6},{8,7},{9,8},{10,9},{11,1... | collective-permute-start | bytes 393224 | tf_op jit(solution)/shard_map/ppermute | solution.py:18
  94.5 86.6 %collective-permute-start.31 = (f32[32,1024]{1,0:T(8,128)S(1)}, f32[32,1024]{1,0:T(8,128)S(1)}, u32[]{:S(2)}, u32[]{:S(2)}) collective-permute-start(f32[32,1024]{1,0:T(8,128)S(1)} %copy-done.8), channel_id=1, source_target_pairs={{2,0},{3,1},{4,2},{5,3},{6,4},{7,5},{8,6},{9,7},{10,8},{11,9},{12,... | collective-permute-start | bytes 393224 | tf_op jit(solution)/shard_map/ppermute | solution.py:18
  98.0 85.3 %collective-permute-start.32 = (f32[32,1024]{1,0:T(8,128)S(1)}, f32[32,1024]{1,0:T(8,128)S(1)}, u32[]{:S(2)}, u32[]{:S(2)}) collective-permute-start(f32[32,1024]{1,0:T(8,128)S(1)} %copy-done.8), channel_id=1, source_target_pairs={{3,0},{4,1},{5,2},{6,3},{7,4},{8,5},{9,6},{10,7},{11,8},{12,9},{13... | collective-permute-start | bytes 393224 | tf_op jit(solution)/shard_map/ppermute | solution.py:18
  100.0 85.3 %collective-permute-start.33 = (f32[32,1024]{1,0:T(8,128)S(1)}, f32[32,1024]{1,0:T(8,128)S(1)}, u32[]{:S(2)}, u32[]{:S(2)}) collective-permute-start(f32[32,1024]{1,0:T(8,128)S(1)} %copy-done.8), channel_id=1, source_target_pairs={{4,0},{5,1},{6,2},{7,3},{8,4},{9,5},{10,6},{11,7},{12,8},{13,9},{1... | collective-permute-start | bytes 393224 | tf_op jit(solution)/shard_map/ppermute | solution.py:18
  106.2 11.0 %collective-permute-start.36 = (f32[32,1024]{1,0:T(8,128)}, f32[32,1024]{1,0:T(8,128)S(1)}, u32[]{:S(2)}, u32[]{:S(2)}) collective-permute-start(f32[32,1024]{1,0:T(8,128)} %param.14), channel_id=1, source_target_pairs={{0,6},{1,7},{2,8},{3,9},{4,10},{5,11},{6,12},{7,13},{8,14},{9,15},... | collective-permute-start | bytes 393224 | tf_op jit(solution)/shard_map/ppermute | solution.py:18
  117.2 15.0 %collective-permute-start.37 = (f32[32,1024]{1,0:T(8,128)}, f32[32,1024]{1,0:T(8,128)S(1)}, u32[]{:S(2)}, u32[]{:S(2)}) collective-permute-start(f32[32,1024]{1,0:T(8,128)} %param.14), channel_id=1, source_target_pairs={{0,5},{1,6},{2,7},{3,8},{4,9},{5,10},{6,11},{7,12},{8,13},{9,14},{... | collective-permute-start | bytes 393224 | tf_op jit(solution)/shard_map/ppermute | solution.py:18
  132.2 11.8 %collective-permute-start.38 = (f32[32,1024]{1,0:T(8,128)}, f32[32,1024]{1,0:T(8,128)S(1)}, u32[]{:S(2)}, u32[]{:S(2)}) collective-permute-start(f32[32,1024]{1,0:T(8,128)} %param.14), channel_id=1, source_target_pairs={{0,4},{1,5},{2,6},{3,7},{4,8},{5,9},{6,10},{7,11},{8,12},{9,13},{1... | collective-permute-start | bytes 393224 | tf_op jit(solution)/shard_map/ppermute | solution.py:18
  144.0 7.6 %collective-permute-start.39 = (f32[32,1024]{1,0:T(8,128)}, f32[32,1024]{1,0:T(8,128)S(1)}, u32[]{:S(2)}, u32[]{:S(2)}) collective-permute-start(f32[32,1024]{1,0:T(8,128)} %param.14), channel_id=1, source_target_pairs={{0,3},{1,4},{2,5},{3,6},{4,7},{5,8},{6,9},{7,10},{8,11},{9,12},{10... | collective-permute-start | bytes 393224 | tf_op jit(solution)/shard_map/ppermute | solution.py:18
  151.7 9.7 %collective-permute-start.40 = (f32[32,1024]{1,0:T(8,128)}, f32[32,1024]{1,0:T(8,128)S(1)}, u32[]{:S(2)}, u32[]{:S(2)}) collective-permute-start(f32[32,1024]{1,0:T(8,128)} %param.14), channel_id=1, source_target_pairs={{0,2},{1,3},{2,4},{3,5},{4,6},{5,7},{6,8},{7,9},{8,10},{9,11},{10,... | collective-permute-start | bytes 393224 | tf_op jit(solution)/shard_map/ppermute | solution.py:18
  161.4 6.5 %collective-permute-start.41 = (f32[32,1024]{1,0:T(8,128)}, f32[32,1024]{1,0:T(8,128)S(1)}, u32[]{:S(2)}, u32[]{:S(2)}) collective-permute-start(f32[32,1024]{1,0:T(8,128)} %param.14), channel_id=1, source_target_pairs={{0,1},{1,2},{2,3},{3,4},{4,5},{5,6},{6,7},{7,8},{8,9},{9,10},{10,1... | collective-permute-start | bytes 393224 | tf_op jit(solution)/shard_map/ppermute | solution.py:18
  167.9 19.4 %collective-permute-start.34 = (f32[32,1024]{1,0:T(8,128)S(1)}, f32[32,1024]{1,0:T(8,128)S(1)}, u32[]{:S(2)}, u32[]{:S(2)}) collective-permute-start(f32[32,1024]{1,0:T(8,128)S(1)} %copy-done.8), channel_id=1, source_target_pairs={{5,0},{6,1},{7,2},{8,3},{9,4},{10,5},{11,6},{12,7},{13,8},{14,9},{... | collective-permute-start | bytes 393224 | tf_op jit(solution)/shard_map/ppermute | solution.py:18
  174.0 16.3 %collective-permute-start.35 = (f32[32,1024]{1,0:T(8,128)S(1)}, f32[32,1024]{1,0:T(8,128)S(1)}, u32[]{:S(2)}, u32[]{:S(2)}) collective-permute-start(f32[32,1024]{1,0:T(8,128)S(1)} %copy-done.8), channel_id=1, source_target_pairs={{6,0},{7,1},{8,2},{9,3},{10,4},{11,5},{12,6},{13,7},{14,8},{15,9},... | collective-permute-start | bytes 393224 | tf_op jit(solution)/shard_map/ppermute | solution.py:18
  181.0 16.6 %collective-permute-start.42 = (f32[32,1024]{1,0:T(8,128)}, f32[32,1024]{1,0:T(8,128)S(1)}, u32[]{:S(2)}, u32[]{:S(2)}) collective-permute-start(f32[32,1024]{1,0:T(8,128)} %param.14), channel_id=1, source_target_pairs={{1,0},{2,1},{3,2},{4,3},{5,4},{6,5},{7,6},{8,7},{9,8},{10,9},{11,1... | collective-permute-start | bytes 393224 | tf_op jit(solution)/shard_map/ppermute | solution.py:18
  183.3 16.6 %collective-permute-start.43 = (f32[32,1024]{1,0:T(8,128)}, f32[32,1024]{1,0:T(8,128)S(1)}, u32[]{:S(2)}, u32[]{:S(2)}) collective-permute-start(f32[32,1024]{1,0:T(8,128)} %param.14), channel_id=1, source_target_pairs={{2,0},{3,1},{4,2},{5,3},{6,4},{7,5},{8,6},{9,7},{10,8},{11,9},{12,... | collective-permute-start | bytes 393224 | tf_op jit(solution)/shard_map/ppermute | solution.py:18
  185.2 21.4 %collective-permute-start.44 = (f32[32,1024]{1,0:T(8,128)}, f32[32,1024]{1,0:T(8,128)S(1)}, u32[]{:S(2)}, u32[]{:S(2)}) collective-permute-start(f32[32,1024]{1,0:T(8,128)} %param.14), channel_id=1, source_target_pairs={{3,0},{4,1},{5,2},{6,3},{7,4},{8,5},{9,6},{10,7},{11,8},{12,9},{13... | collective-permute-start | bytes 393224 | tf_op jit(solution)/shard_map/ppermute | solution.py:18
  187.3 23.1 %collective-permute-start.45 = (f32[32,1024]{1,0:T(8,128)}, f32[32,1024]{1,0:T(8,128)S(1)}, u32[]{:S(2)}, u32[]{:S(2)}) collective-permute-start(f32[32,1024]{1,0:T(8,128)} %param.14), channel_id=1, source_target_pairs={{4,0},{5,1},{6,2},{7,3},{8,4},{9,5},{10,6},{11,7},{12,8},{13,9},{1... | collective-permute-start | bytes 393224 | tf_op jit(solution)/shard_map/ppermute | solution.py:18
  190.3 25.0 %collective-permute-start.46 = (f32[32,1024]{1,0:T(8,128)}, f32[32,1024]{1,0:T(8,128)S(1)}, u32[]{:S(2)}, u32[]{:S(2)}) collective-permute-start(f32[32,1024]{1,0:T(8,128)} %param.14), channel_id=1, source_target_pairs={{5,0},{6,1},{7,2},{8,3},{9,4},{10,5},{11,6},{12,7},{13,8},{14,9},{... | collective-permute-start | bytes 393224 | tf_op jit(solution)/shard_map/ppermute | solution.py:18
  197.7 31.3 %collective-permute-start.47 = (f32[32,1024]{1,0:T(8,128)}, f32[32,1024]{1,0:T(8,128)S(1)}, u32[]{:S(2)}, u32[]{:S(2)}) collective-permute-start(f32[32,1024]{1,0:T(8,128)} %param.14), channel_id=1, source_target_pairs={{6,0},{7,1},{8,2},{9,3},{10,4},{11,5},{12,6},{13,7},{14,8},{15,9},... | collective-permute-start | bytes 393224 | tf_op jit(solution)/shard_map/ppermute | solution.py:18
  199.9 144.3 %collective-permute-start.16 = (f32[32,256]{1,0:T(8,128)}, f32[32,256]{1,0:T(8,128)}, u32[]{:S(2)}, u32[]{:S(2)}) collective-permute-start(f32[32,256]{1,0:T(8,128)} %get-tuple-element.496), channel_id=1, source_target_pairs={{0,8},{1,9},{2,10},{3,11},{4,12},{5,13},{6,14},{7,15},{8,0},{9,1},... | collective-permute-start | bytes 98312 | tf_op jit(solution)/shard_map/ppermute | solution.py:24
  206.6 146.8 %collective-permute-start.13 = (f32[32,256]{1,0:T(8,128)}, f32[32,256]{1,0:T(8,128)}, u32[]{:S(2)}, u32[]{:S(2)}) collective-permute-start(f32[32,256]{1,0:T(8,128)} %fusion.75), channel_id=1, source_target_pairs={{0,8},{1,9},{2,10},{3,11},{4,12},{5,13},{6,14},{7,15},{8,0},{9,1},... | collective-permute-start | bytes 98312 | tf_op jit(solution)/shard_map/ppermute | solution.py:24
  210.4 156.6 %collective-permute-start.21 = (f32[32,256]{0,1:T(8,128)}, f32[32,256]{0,1:T(8,128)}, u32[]{:S(2)}, u32[]{:S(2)}) collective-permute-start(f32[32,256]{0,1:T(8,128)} %get-tuple-element.494), channel_id=1, source_target_pairs={{0,8},{1,9},{2,10},{3,11},{4,12},{5,13},{6,14},{7,15},{8,0},{9,1},... | collective-permute-start | bytes 98312 | tf_op jit(solution)/shard_map/ppermute | solution.py:24
  215.3 153.1 %collective-permute-start.22 = (f32[32,256]{0,1:T(8,128)}, f32[32,256]{0,1:T(8,128)}, u32[]{:S(2)}, u32[]{:S(2)}) collective-permute-start(f32[32,256]{0,1:T(8,128)} %get-tuple-element.494), channel_id=1, source_target_pairs={{0,16},{1,17},{2,18},{3,19},{4,20},{5,21},{6,22},{7,23},{8,24},{9,... | collective-permute-start | bytes 98312 | tf_op jit(solution)/shard_map/ppermute | solution.py:24
  229.0 115.3 %collective-permute-start.17 = (f32[32,256]{1,0:T(8,128)}, f32[32,256]{1,0:T(8,128)}, u32[]{:S(2)}, u32[]{:S(2)}) collective-permute-start(f32[32,256]{1,0:T(8,128)} %collective-permute-done.15), channel_id=1, source_target_pairs={{0,8},{1,9},{2,10},{3,11},{4,12},{5,13},{6,14},{7,15},{8,0},{9,1},... | collective-permute-start | bytes 98312 | tf_op jit(solution)/shard_map/ppermute | solution.py:24
  344.3 25.1 %collective-permute-start.18 = (f32[32,256]{1,0:T(8,128)}, f32[32,256]{1,0:T(8,128)S(1)}, u32[]{:S(2)}, u32[]{:S(2)}) collective-permute-start(f32[32,256]{1,0:T(8,128)} %fusion.71), channel_id=1, source_target_pairs={{0,8},{1,9},{2,10},{3,11},{4,12},{5,13},{6,14},{7,15},{8,0},{9,1},... | collective-permute-start | bytes 98312 | tf_op jit(solution)/shard_map/ppermute | solution.py:24
  344.3 21.9 %collective-permute-start.14 = (f32[32,256]{1,0:T(8,128)}, f32[32,256]{1,0:T(8,128)S(1)}, u32[]{:S(2)}, u32[]{:S(2)}) collective-permute-start(f32[32,256]{1,0:T(8,128)} %copy-done.16), channel_id=1, source_target_pairs={{0,8},{1,9},{2,10},{3,11},{4,12},{5,13},{6,14},{7,15},{8,0},{9,1},... | collective-permute-start | bytes 98312 | tf_op jit(solution)/shard_map/ppermute | solution.py:24
  353.5 21.6 %collective-permute-start.19 = (f32[32,256]{1,0:T(8,128)}, f32[32,256]{1,0:T(8,128)S(1)}, u32[]{:S(2)}, u32[]{:S(2)}) collective-permute-start(f32[32,256]{1,0:T(8,128)} %fusion.71), channel_id=1, source_target_pairs={{0,16},{1,17},{2,18},{3,19},{4,20},{5,21},{6,22},{7,23},{8,24},{9,... | collective-permute-start | bytes 98312 | tf_op jit(solution)/shard_map/ppermute | solution.py:24
  367.0 5.3 %collective-permute-start.23 = (f32[32,256]{0,1:T(8,128)}, f32[32,256]{0,1:T(8,128)S(1)}, u32[]{:S(2)}, u32[]{:S(2)}) collective-permute-start(f32[32,256]{0,1:T(8,128)} %collective-permute-done.21), channel_id=1, source_target_pairs={{0,16},{1,17},{2,18},{3,19},{4,20},{5,21},{6,22},{7,23},{8,24},{9,... | collective-permute-start | bytes 98312 | tf_op jit(solution)/shard_map/ppermute | solution.py:24
  369.4 5.6 %collective-permute-start.20 = (f32[32,256]{1,0:T(8,128)S(1)}, f32[32,256]{1,0:T(8,128)S(1)}, u32[]{:S(2)}, u32[]{:S(2)}) collective-permute-start(f32[32,256]{1,0:T(8,128)S(1)} %collective-permute-done.18), channel_id=1, source_target_pairs={{0,16},{1,17},{2,18},{3,19},{4,20},{5,21},{6,22},{7,23},{8,24},{9,... | collective-permute-start | bytes 98312 | tf_op jit(solution)/shard_map/ppermute | solution.py:24
  (70 other events, 419.9 us)
where the time goes:
time: 384 us; the launch traced here: 382 us
  starting transfers between devices  149 us (39%)
  matrix products  120 us (31%)
  waiting for transfers between devices  62 us (16%)
  local copies, waits for them, and re-layouts  23.2 us (6%)
  between operations  15.6 us (4%)
  other arithmetic  10.6 us (3%)
    ppermute x24, starting transfers between devices, shifted(): lax.ppermute(value, axis, [(source, source + steps) for source in range(l...  90.6 us
    dot_general x64, matrix products, kernel(): lax.dot_general(left_set, right_set, (((0,), (0,)), ((), ())), precision=...  60.2 us
    ppermute x24, starting transfers between devices, partner(): return lax.ppermute(value, axis, pairs)  58.1 us
    dot_general x68, matrix products, apply_rows(): lax.dot_general(weights, kernel_tile, (((1,), (1,)), ((), ())), precision...  56.7 us
    ppermute x24, waiting for transfers between devices, shifted(): lax.ppermute(value, axis, [(source, source + steps) for source in range(l...  47.9 us
    ppermute x24, waiting for transfers between devices, partner(): return lax.ppermute(value, axis, pairs)  14.1 us
  transfers between devices with their start and end apart: 48, of which 17 were waited for; matrix products, arithmetic and copies ran while one was open for 38% of the time, Pallas kernels for 0%

commit v1 on v0

v1 whole, which is shorter than its diff:
```python
import functools
import math
import jax
import jax.numpy as jnp
from jax import lax
from jax.experimental import pallas as pl
from jax.experimental.pallas import tpu as pltpu
from jax.sharding import PartitionSpec as P

RANK = 256
LEVELS = 4
BLOCK = 256

f32 = jnp.float32
bf16 = jnp.bfloat16
SCALE = math.log2(math.e) / 16.0
NN = (((1,), (0,)), ((), ()))
NT = (((1,), (1,)), ((), ()))
VMEM = pl.BlockSpec(memory_space=pltpu.VMEM)
ANY = pl.BlockSpec(memory_space=pl.ANY)
HBM = pl.BlockSpec(memory_space=pltpu.HBM)


def mm(left, right, dims=NN):
    return lax.dot_general(left, right, dims, preferred_element_type=f32)


def split2(value):
    high = value.astype(bf16)
    return high, (value - high.astype(f32)).astype(bf16)


def split3(value):
    high = value.astype(bf16)
    rest = value - high.astype(f32)
    middle = rest.astype(bf16)
    return high, middle, (rest - middle.astype(f32)).astype(bf16)


def stack3(value):
    return jnp.concatenate(split3(value), axis=0)


def sum3(value):
    rows = value.shape[0] // 3
    return value[:rows] + value[rows : 2 * rows] + value[2 * rows :]


def norm_rows(value, first):
    count = value.shape[1]
    parts = split3(-SCALE * jnp.sum(value * value, axis=0, keepdims=True))
    parts = [part.astype(f32) for part in parts]
    ones = jnp.ones((3, count), f32)
    pad = jnp.zeros((10, count), f32)
    order = [*parts, ones, pad] if first else [ones, *parts, pad]
    return jnp.concatenate(order, axis=0).astype(bf16)


def own_features(points):
    a, b, c = split3(points * (2.0 * SCALE))
    return jnp.concatenate([a, a, b, b, a, c, norm_rows(points, True)], axis=0)


def other_features(points):
    a, b, c = split3(points)
    return jnp.concatenate([a, b, a, b, c, a, norm_rows(points, False)], axis=0)


def kernel_pieces(other, own):
    return split2(jnp.exp2(mm(other, own)))


def add_tile(other_points, other_charges, feature_ref, total_ref):
    other = other_features(other_points).T
    weights = stack3(other_charges)
    size = feature_ref.shape[1]
    for column in range(0, size, BLOCK):
        own = feature_ref[:, column : column + BLOCK]
        total = total_ref[:, column : column + BLOCK]
        for row in range(0, size, BLOCK):
            high, low = kernel_pieces(other[row : row + BLOCK], own)
            part = weights[:, row : row + BLOCK]
            total = total + mm(part, high) + mm(part, low)
        total_ref[:, column : column + BLOCK] = total


def pair(points, charges, other_points, other_charges, out):
    half = points.shape[0]
    for place, part in enumerate((points, charges, other_points, other_charges)):
        out[half * place : half * (place + 1)] = part[...]


def leaf_node(chip, chosen, matrix, out):
    size = chip.shape[1]
    spots = lax.broadcasted_iota(jnp.int32, (size, RANK), 0)
    marks = (spots == chosen[...]).astype(f32).astype(bf16)
    out[:32] = sum3(mm(stack3(chip[:32]), marks))
    high, low = split2(matrix[0])
    weights = stack3(chip[32:64])
    out[32:] = sum3(mm(weights, high, NT) + mm(weights, low, NT))


def near_first(near, chip, token, near_out, features, total):
    size = total.shape[1]
    me = lax.axis_index("leaf")
    features[...] = own_features(chip[:32])
    total[...] = jnp.zeros_like(total)
    add_tile(chip[:32], chip[32:64], features, total)
    sibling = me + 1 - 2 * lax.rem(me, 2)
    wanted = jnp.sum((near[...] == sibling).astype(jnp.int32))

    @pl.when(wanted > 0)
    def _():
        add_tile(chip[64:96], chip[96:], features, total)

    near_out[...] = sum3(total[...])


def near_blocks(entries, count, near, near_in, features, token, *refs):
    sources = refs[:count]
    near_out, slots, total, sems = refs[count:]
    me = lax.axis_index("leaf")
    sign = 2 * lax.rem(me, 2) - 1
    wanted = jnp.sum(lax.shift_left(jnp.int32(1), near[...] - me + 6))
    taken = jnp.int32(0)
    for source, row, offset in entries:
        bit = lax.rem(lax.shift_right_logical(wanted, sign * offset + 6), 2)

        @pl.when(bit == 1)
        def _(source=source, row=row, slot=taken):
            pltpu.make_async_copy(
                sources[source].at[pl.ds(row, 64)], slots.at[slot], sems.at[slot]
            ).start()

        taken = taken + bit
    total[...] = jnp.zeros_like(total)

    def step(slot, carry):
        pltpu.make_async_copy(
            sources[0].at[pl.ds(0, 64)], slots.at[slot], sems.at[slot]
        ).wait()
        add_tile(slots[slot, :32], slots[slot, 32:], features, total)
        return carry

    lax.fori_loop(0, taken, step, 0)
    near_out[...] = near_in[...] + sum3(total[...])


def merge(level, own, sibling, chosen, matrix, token, sent, extra=None):
    me = lax.axis_index("leaf")
    right = lax.rem(lax.shift_right_logical(me, level), 2)
    kind = lax.rem(me, 2)
    if level == 0:
        rows = pl.ds(pl.multiple_of(kind * 32, 32), 32)
        mine = own[rows, :]
        theirs = sibling[rows, :]
    else:
        mine = own[:, 2 * RANK :]
        theirs = sibling[:, 2 * RANK :]
        extra[:, : 2 * RANK] = sibling[:, : 2 * RANK]
        extra[:, 2 * RANK : 3 * RANK] = mine
        extra[:, 3 * RANK :] = theirs
    sent[:, :RANK] = mine
    sent[:, RANK : 2 * RANK] = theirs
    if level == LEVELS - 1:
        return
    mine = stack3(mine)
    theirs = stack3(theirs)
    first = right * RANK
    second = RANK - first

    @pl.when(kind == 0)
    def _():
        spots = lax.broadcasted_iota(jnp.int32, (RANK, RANK), 0)
        row = chosen[level]
        left_marks = (spots + first == row).astype(f32).astype(bf16)
        right_marks = (spots + second == row).astype(f32).astype(bf16)
        sent[:, 2 * RANK :] = sum3(mm(mine, left_marks) + mm(theirs, right_marks))

    @pl.when(kind == 1)
    def _():
        near_high, near_low = split2(
            matrix[0, level, :, pl.ds(pl.multiple_of(first, RANK), RANK)]
        )
        far_high, far_low = split2(
            matrix[0, level, :, pl.ds(pl.multiple_of(second, RANK), RANK)]
        )
        sent[:, 2 * RANK :] = sum3(
            (mm(mine, near_high, NT) + mm(mine, near_low, NT))
            + (mm(theirs, far_high, NT) + mm(theirs, far_low, NT))
        )


def sorted_kinds(pair, mine, theirs):
    kind = lax.rem(lax.axis_index("leaf"), 2)
    left = pair[0][:, RANK * mine : RANK * (mine + 1)]
    right = pair[1][:, RANK * theirs : RANK * (theirs + 1)]
    return jnp.where(kind == 0, left, right), jnp.where(kind == 0, right, left)


def far_level(level, codes, own, choices):
    picked = []
    for position in range(2):
        code = codes[0, position : position + 1, level : level + 1]
        picked.append(
            [
                jnp.where(code == 1, one, jnp.where(code == 2, two, three))
                for one, two, three in zip(*choices, strict=True)
            ]
        )
    others = jnp.concatenate([picked[0][0], picked[1][0]], axis=1)
    weights = stack3(jnp.concatenate([picked[0][1], picked[1][1]], axis=1))
    high, low = kernel_pieces(other_features(others).T, own_features(own))
    return sum3(mm(weights, high) + mm(weights, low))


def far_lower(codes, leaf_own, leaf_sibling, *refs):
    kept = [refs[0:2], refs[2:4], refs[4:6]]
    out = refs[6]
    choices = [
        (leaf_sibling[:32], leaf_sibling[32:]),
        sorted_kinds(kept[0], 0, 1),
        sorted_kinds(kept[0], 1, 0),
    ]
    out[:32] = far_level(0, codes, leaf_own[:32], choices)
    for level in (1, 2):
        choices = [
            sorted_kinds(kept[level - 1], 3, 3),
            sorted_kinds(kept[level], 0, 0),
            sorted_kinds(kept[level], 1, 1),
        ]
        own = sorted_kinds(kept[level - 1], 2, 2)[0]
        out[32 * level : 32 * level + 32] = far_level(level, codes, own, choices)


def finish(
    codes, gain, chip, leaf_matrix, upper_matrix, near_field, lower, kept, kept_other, last, last_other, out
):
    me = lax.axis_index("leaf")
    kept = (kept, kept_other)
    last = (last, last_other)
    choices = [sorted_kinds(kept, 3, 3), sorted_kinds(last, 0, 0), sorted_kinds(last, 1, 1)]
    local = far_level(3, codes, sorted_kinds(kept, 2, 2)[0], choices)
    for level in reversed(range(LEVELS - 1)):
        right = lax.rem(lax.shift_right_logical(me, level), 2)
        columns = pl.ds(pl.multiple_of(right * RANK, RANK), RANK)
        half = upper_matrix[0, level, :, columns]
        high, low = split2(half)
        pieces = stack3(local)
        local = lower[32 * level : 32 * level + 32] + sum3(mm(pieces, high) + mm(pieces, low))
    high, low = split2(leaf_matrix[0])
    pieces = stack3(local)
    far_out = sum3(mm(pieces, high) + mm(pieces, low))
    count = gain.shape[1]
    diagonal = lax.broadcasted_iota(jnp.int32, (count, count), 0) == lax.broadcasted_iota(
        jnp.int32, (count, count), 1
    )
    column = jnp.sum(jnp.where(diagonal, gain[...], 0.0), axis=1, keepdims=True)
    out[...] = far_out + near_field[...] + column * chip[32:64]


def call(function, shapes, in_specs, flops, scratch=(), limit=16, **extra):
    many = isinstance(shapes, list)
    return pl.pallas_call(
        function,
        out_shape=shapes,
        in_specs=in_specs,
        out_specs=[VMEM] * len(shapes) if many else VMEM,
        scratch_shapes=list(scratch),
        cost_estimate=pl.CostEstimate(flops=flops, bytes_accessed=1 << 20, transcendentals=0),
        compiler_params=pltpu.CompilerParams(vmem_limit_bytes=limit << 20),
        **extra,
    )


def gate(value, token, out):
    pass


def after(value, token):
    return pl.pallas_call(
        gate,
        out_shape=shape(*value.shape),
        in_specs=[ANY, ANY],
        out_specs=ANY,
        input_output_aliases={0: 0},
        compiler_params=pltpu.CompilerParams(vmem_limit_bytes=1 << 20),
    )(value, token)


def shape(rows, columns, kind=f32):
    return jax.ShapeDtypeStruct((rows, columns), kind)


def body(
    points,
    charges,
    leaf_skeleton,
    upper_skeleton,
    leaf_projection,
    upper_projection,
    near_leaves,
    far_codes,
    regularizer,
):
    devices = lax.axis_size("leaf")
    size = points.shape[1]

    def partner(value, bit):
        return lax.ppermute(value, "leaf", [(leaf, leaf ^ (1 << bit)) for leaf in range(devices)])

    def along(value, chips):
        pairs = [(leaf, leaf + 2 * chips * (1 - 2 * (leaf % 2))) for leaf in range(devices)]
        pairs = [(source, target) for source, target in pairs if 0 <= target < devices]
        return lax.ppermute(value, "leaf", pairs)

    def near_step(near_field, token, sources, entries):
        count = len(sources)
        return call(
            functools.partial(near_blocks, entries, count),
            shape(32, size),
            [VMEM] * 3 + [ANY] * (1 + count),
            4 * 10**10,
            [
                pltpu.VMEM((len(entries), 64, size), f32),
                pltpu.VMEM((96, size), f32),
                pltpu.SemaphoreType.DMA((len(entries),)),
            ],
        )(near_leaves, near_field, features, token, *sources)

    def merge_step(level, own, sibling, token):
        shapes = [shape(32, (3 if level < LEVELS - 1 else 2) * RANK)]
        if level > 0:
            shapes.append(shape(32, 4 * RANK))
        return call(functools.partial(merge, level), shapes, [VMEM] * 4 + [ANY], 10**8)(
            own, sibling, upper_chosen, upper_projection, token
        )

    upper_chosen = jnp.transpose(upper_skeleton, (1, 0, 2))
    codes = jnp.transpose(far_codes, (0, 2, 1))

    chip = call(pair, shape(128, size), [VMEM] * 4, 10**8)(
        points, charges, partner(points, 0), partner(charges, 0)
    )
    got2 = along(chip, 2)
    got1 = along(chip, 1)
    node = call(leaf_node, shape(64, RANK), [VMEM] * 3, 10**11)(
        chip, leaf_skeleton, leaf_projection
    )
    sibling_node = partner(node, 0)
    (sent1,) = merge_step(0, node, sibling_node, node)
    far1 = partner(sent1, 1)
    near_field, features = call(
        near_first,
        [shape(32, size), shape(208, size, bf16)],
        [VMEM] * 2 + [ANY],
        2 * 10**9,
        [pltpu.VMEM((96, size), f32)],
    )(near_leaves, chip, sent1)
    got2 = after(got2, near_field)
    sent2, kept2 = merge_step(1, sent1, far1, got2)
    far2 = partner(sent2, 2)
    kept2_other = partner(kept2, 0)
    got3 = along(got2, 1)
    other2 = partner(got2, 0)
    sent3, kept3 = merge_step(2, sent2, far2, near_field)
    far3 = partner(sent3, 3)
    kept3_other = partner(kept3, 0)
    got1 = after(got1, sent2)
    other1 = partner(got1, 0)
    entries = [(0, 0, 4), (0, 64, 3), (1, 0, -5), (1, 64, -4)]
    entries += [(2, 0, 2), (2, 64, 1), (3, 0, -3), (3, 64, -2)]
    near_field = near_step(near_field, sent3, [got2, other2, got1, other1], entries)
    sent4, kept4 = merge_step(3, sent3, far3, near_field)
    far4 = partner(sent4, 4)
    kept4_other = partner(kept4, 0)
    got3 = after(got3, near_field)
    other3 = partner(got3, 0)
    lower = call(far_lower, shape(96, RANK), [VMEM] * 9, 10**10)(
        codes, node, sibling_node, kept2, kept2_other, kept3, kept3_other, kept4, kept4_other
    )
    far4_other = partner(after(far4, lower), 0)
    entries = [(0, 0, 6), (0, 64, 5), (1, 64, -6)]
    near_field = near_step(near_field, lower, [got3, other3], entries)
    return call(finish, shape(32, size), [VMEM] * 11, 10**9)(
        codes,
        regularizer[None, :],
        chip,
        leaf_projection,
        upper_projection,
        near_field,
        lower,
        kept4,
        kept4_other,
        far4,
        far4_other,
    )


def solution(mesh):
    placed = (
        P(None, "leaf"),
        P(None, "leaf"),
        P("leaf", None),
        P("leaf", None, None),
        P("leaf", None, None),
        P("leaf", None, None, None),
        P("leaf", None),
        P("leaf", None, None),
        P(),
    )
    return jax.shard_map(
        body, mesh=mesh, in_specs=placed, out_specs=P(None, "leaf"), check_vma=False
    )
```

time: 384 us -> 65.1 us (0.17)
  the two profiles are of different devices: /device:TPU:100 before, /device:TPU:24 now
where the time goes in v1:
time: 65.1 us; the launch traced here: 64.5 us
  starting transfers between devices  30.1 us (46%)
  Pallas kernels  15.6 us (24%)
  waiting for transfers between devices  14.8 us (23%)
  local copies, waits for them, and re-layouts  3.79 us (6%)
    ppermute x14, starting transfers between devices, partner(): lax.ppermute(value, 'leaf', [(leaf, leaf ^ 1 << bit) for leaf in range(de...  16.6 us
    ppermute x3, starting transfers between devices, along(): return lax.ppermute(value, 'leaf', pairs)  13.5 us
    ppermute x14, waiting for transfers between devices, partner(): lax.ppermute(value, 'leaf', [(leaf, leaf ^ 1 << bit) for leaf in range(de...  11.5 us
    pallas_call x2, Pallas kernels, near_step(): call(functools.partial(near_blocks, entries, count), shape(32, size), [VM...  9.91 us
    unnamed x21, local copies, waits for them, and re-layouts  3.79 us
    ppermute x3, waiting for transfers between devices, along(): return lax.ppermute(value, 'leaf', pairs)  3.25 us
    pallas_call x1, Pallas kernels, body(): call(finish, shape(32, size), [VMEM] * 11, 10 ** 9)  2.18 us
    pallas_call x1, Pallas kernels, body(): call(near_first, [shape(32, size), shape(208, size, bf16)], [VMEM] * 2 +...  1.55 us
  transfers between devices with their start and end apart: 17, of which 9 were waited for; matrix products, arithmetic and copies ran while one was open for 0% of the time, Pallas kernels for 21%

profile of v1, /device:TPU:24, one launch (start us, length us, event | category | flops | bytes accessed | tf_op | source)
XLA Modules:
  0.0 64.5 jit_solution(5050458253951746449)
XLA Ops:
  0.0 0.0 collective-permute-start
  0.0 0.5 collective-permute-start.1
  0.5 1.0 %collective-permute-done.other_points = f32[32,1024]{1,0:T(8,128)S(1)} collective-permute-done((f32[32,1024]{1,0:T(8,128)}, f32[32,1024]{1,0:T(8,128)S(1)}, u32[]{:S(2)}, u32[]{:S(2)}) %collective-permute-start) | collective-permute-done | bytes 131104 | tf_op jit(solution)/shard_map/ppermute | solution.py:310
  1.6 0.2 collective-permute-done.1.other_charges
  1.7 0.9 %copy-done.3 = f32[32,1024]{1,0:T(8,128)S(1)} copy-done((f32[32,1024]{1,0:T(8,128)S(1)}, f32[32,1024]{1,0:T(8,128)}, u32[]{:S(2)}) %copy-start.3) | copy-done | bytes 131096
  2.7 0.9 %copy-done.4 = f32[32,1024]{1,0:T(8,128)S(1)} copy-done((f32[32,1024]{1,0:T(8,128)S(1)}, f32[32,1024]{1,0:T(8,128)}, u32[]{:S(2)}) %copy-start.4) | copy-done | bytes 131096
  3.6 0.0 copy-start
  3.6 5.3 %collective-permute-start.4 = (f32[128,1024]{1,0:T(8,128)S(1)}, f32[128,1024]{1,0:T(8,128)S(1)}, u32[]{:S(2)}, u32[]{:S(2)}) collective-permute-start(f32[128,1024]{1,0:T(8,128)S(1)} %shard_map.91.chip), channel_id=1, source_target_pairs={{0,4},{2,6},{4,8},{5,1},{6,10},{7,3},{8,12},{9,5},{10,14},{11,7},{... | collective-permute-start | bytes 1572872 | tf_op jit(solution)/shard_map/ppermute | solution.py:315
  8.9 3.8 %collective-permute-start.7 = (f32[128,1024]{1,0:T(8,128)S(1)}, f32[128,1024]{1,0:T(8,128)S(1)}, u32[]{:S(2)}, u32[]{:S(2)}) collective-permute-start(f32[128,1024]{1,0:T(8,128)S(1)} %shard_map.91.chip), channel_id=1, source_target_pairs={{0,2},{2,4},{3,1},{4,6},{5,3},{6,8},{7,5},{8,10},{9,7},{10,12},{11... | collective-permute-start | bytes 1572872 | tf_op jit(solution)/shard_map/ppermute | solution.py:315
  12.8 0.0 copy-start.1
  12.8 1.2 %copy-done.1 = f32[1,256,1024]{2,1,0:T(8,128)S(1)} copy-done((f32[1,256,1024]{2,1,0:T(8,128)S(1)}, f32[1,256,1024]{2,1,0:T(8,128)}, u32[]{:S(2)}) %copy-start.1) | copy-done | bytes 1048600
  14.0 0.7 %copy-done.8 = s32[1,256]{1,0:T(1,128)S(1)} copy-done((s32[1,256]{1,0:T(1,128)S(1)}, s32[1,256]{1,0:T(1,128)}, u32[]{:S(2)}) %copy-start.8) | copy-done | bytes 1048
  14.7 0.5 shard_map.92.own.token.leaf_own
  15.2 0.0 copy-start.9
  15.2 4.3 %collective-permute-start.2 = (f32[64,256]{1,0:T(8,128)S(1)}, f32[64,256]{1,0:T(8,128)S(1)}, u32[]{:S(2)}, u32[]{:S(2)}) collective-permute-start(f32[64,256]{1,0:T(8,128)S(1)} %shard_map.92.own.token.leaf_own), channel_id=1, source_target_pairs={{0,1},{1,0},{2,3},{3,2},{4,5},{5,4},{6,7},{7,6},{8,9},{9,8},{10,11... | collective-permute-start | bytes 196616 | tf_op jit(solution)/shard_map/ppermute | solution.py:310
  19.6 0.9 %collective-permute-done.2.sibling.leaf_sibling = f32[64,256]{1,0:T(8,128)S(1)} collective-permute-done((f32[64,256]{1,0:T(8,128)S(1)}, f32[64,256]{1,0:T(8,128)S(1)}, u32[]{:S(2)}, u32[]{:S(2)}) %collective-permute-start.2) | collective-permute-done | bytes 65568 | tf_op jit(solution)/shard_map/ppermute | solution.py:310
  20.5 0.2 shard_map.93.token.own
  20.6 1.1 %collective-permute-start.3 = (f32[32,768]{1,0:T(8,128)S(1)}, f32[32,768]{1,0:T(8,128)S(1)}, u32[]{:S(2)}, u32[]{:S(2)}) collective-permute-start(f32[32,768]{1,0:T(8,128)S(1)} %shard_map.93.token.own), channel_id=1, source_target_pairs={{0,2},{1,3},{2,0},{3,1},{4,6},{5,7},{6,4},{7,5},{8,10},{9,11},{10,... | collective-permute-start | bytes 294920 | tf_op jit(solution)/shard_map/ppermute | solution.py:310
  21.7 1.5 %shard_map.94 = (f32[32,1024]{1,0:T(8,128)S(1)}, bf16[208,1024]{1,0:T(8,128)(2,1)S(1)}) custom-call(s32[1,7]{1,0:T(1,128)S(1)} %copy-done.9, f32[128,1024]{1,0:T(8,128)S(1)} %shard_map.91.chip, f32[32,768]{1,0:T(8,128)S(1)} %shard_map.93.token.own), custom_call_target="tpu_custom_call" | custom-call | flops 2000000000 | bytes 1048576 | tf_op jit(solution)/shard_map/pallas_call | solution.py:353
  23.3 0.2 collective-permute-done.4.value
  23.4 5.6 %collective-permute-done.3.sibling = f32[32,768]{1,0:T(8,128)S(1)} collective-permute-done((f32[32,768]{1,0:T(8,128)S(1)}, f32[32,768]{1,0:T(8,128)S(1)}, u32[]{:S(2)}, u32[]{:S(2)}) %collective-permute-start.3) | collective-permute-done | bytes 98336 | tf_op jit(solution)/shard_map/ppermute | solution.py:310
  29.0 0.2 shard_map.96
  29.2 3.1 %collective-permute-done.7.value = f32[128,1024]{1,0:T(8,128)S(1)} collective-permute-done((f32[128,1024]{1,0:T(8,128)S(1)}, f32[128,1024]{1,0:T(8,128)S(1)}, u32[]{:S(2)}, u32[]{:S(2)}) %collective-permute-start.7) | collective-permute-done | bytes 524320 | tf_op jit(solution)/shard_map/ppermute | solution.py:315
  32.3 0.9 %collective-permute-start.8 = (f32[128,1024]{1,0:T(8,128)S(1)}, f32[128,1024]{1,0:T(8,128)S(1)}, u32[]{:S(2)}, u32[]{:S(2)}) collective-permute-start(f32[128,1024]{1,0:T(8,128)S(1)} %shard_map.98.refs_2_), channel_id=1, source_target_pairs={{0,1},{1,0},{2,3},{3,2},{4,5},{5,4},{6,7},{7,6},{8,9},{9,8},{10,11... | collective-permute-start | bytes 1572872 | tf_op jit(solution)/shard_map/ppermute | solution.py:310
  33.2 0.1 collective-permute-start.6
  33.3 0.9 %collective-permute-start.5 = (f32[32,768]{1,0:T(8,128)S(1)}, f32[32,768]{1,0:T(8,128)S(1)}, u32[]{:S(2)}, u32[]{:S(2)}) collective-permute-start(f32[32,768]{1,0:T(8,128)S(1)} %get-tuple-element.15.own.token), channel_id=1, source_target_pairs={{0,4},{1,5},{2,6},{3,7},{4,0},{5,1},{6,2},{7,3},{8,12},{9,13},{10,... | collective-permute-start | bytes 294920 | tf_op jit(solution)/shard_map/ppermute | solution.py:310
  34.2 4.4 %collective-permute-start.13 = (f32[128,1024]{1,0:T(8,128)S(1)}, f32[128,1024]{1,0:T(8,128)S(1)}, u32[]{:S(2)}, u32[]{:S(2)}) collective-permute-start(f32[128,1024]{1,0:T(8,128)S(1)} %shard_map.95.token.refs_0_), channel_id=1, source_target_pairs={{0,2},{2,4},{3,1},{4,6},{5,3},{6,8},{7,5},{8,10},{9,7},{10,12},{11... | collective-permute-start | bytes 1572872 | tf_op jit(solution)/shard_map/ppermute | solution.py:315
  38.5 2.2 %collective-permute-start.9 = (f32[32,1024]{1,0:T(8,128)S(1)}, f32[32,1024]{1,0:T(8,128)S(1)}, u32[]{:S(2)}, u32[]{:S(2)}) collective-permute-start(f32[32,1024]{1,0:T(8,128)S(1)} %get-tuple-element.17.refs_0_), channel_id=1, source_target_pairs={{0,1},{1,0},{2,3},{3,2},{4,5},{5,4},{6,7},{7,6},{8,9},{9,8},{10,11... | collective-permute-start | bytes 393224 | tf_op jit(solution)/shard_map/ppermute | solution.py:310
  40.7 0.6 %collective-permute-done.5.sibling = f32[32,768]{1,0:T(8,128)S(1)} collective-permute-done((f32[32,768]{1,0:T(8,128)S(1)}, f32[32,768]{1,0:T(8,128)S(1)}, u32[]{:S(2)}, u32[]{:S(2)}) %collective-permute-start.5) | collective-permute-done | bytes 98336 | tf_op jit(solution)/shard_map/ppermute | solution.py:310
  41.3 0.2 shard_map.97
  41.5 2.0 %collective-permute-start.11 = (f32[32,768]{1,0:T(8,128)S(1)}, f32[32,768]{1,0:T(8,128)S(1)}, u32[]{:S(2)}, u32[]{:S(2)}) collective-permute-start(f32[32,768]{1,0:T(8,128)S(1)} %get-tuple-element.16.token.own), channel_id=1, source_target_pairs={{0,8},{1,9},{2,10},{3,11},{4,12},{5,13},{6,14},{7,15},{8,0},{9,1},... | collective-permute-start | bytes 294920 | tf_op jit(solution)/shard_map/ppermute | solution.py:310
  43.5 0.0 collective-permute-done.8.refs_3_
  43.5 0.0 collective-permute-start.10
  43.5 0.0 collective-permute-done.6.refs_1_
  43.5 6.5 %shard_map.99.token.near_in = f32[32,1024]{1,0:T(8,128)S(1)} custom-call(s32[1,7]{1,0:T(1,128)S(1)} %copy-done.9, f32[32,1024]{1,0:T(8,128)S(1)} %get-tuple-element.13.token.near_in, bf16[208,1024]{1,0:T(8,128)(2,1)S(1)} %get-tuple-element.14.features, f32[32,768]{1,0:T(8,128)S(1)} %get-tuple-element.16.token.own, f32[128,1024]{1,0:T(8,128)S(1)} %shard_map.95.token.refs_0_, ...), custom_call_target="tpu_custom_call" | custom-call | flops 40000000000 | bytes 1048576 | tf_op jit(solution)/shard_map/pallas_call | solution.py:319
  50.1 0.0 copy-start.6
  50.1 0.8 %collective-permute-done.11.sibling = f32[32,768]{1,0:T(8,128)S(1)} collective-permute-done((f32[32,768]{1,0:T(8,128)S(1)}, f32[32,768]{1,0:T(8,128)S(1)}, u32[]{:S(2)}, u32[]{:S(2)}) %collective-permute-start.11) | collective-permute-done | bytes 98336 | tf_op jit(solution)/shard_map/ppermute | solution.py:310
  50.9 1.5 %collective-permute-start.12 = (f32[32,1024]{1,0:T(8,128)S(1)}, f32[32,1024]{1,0:T(8,128)S(1)}, u32[]{:S(2)}, u32[]{:S(2)}) collective-permute-start(f32[32,1024]{1,0:T(8,128)S(1)} %get-tuple-element.19.refs_4_.kept), channel_id=1, source_target_pairs={{0,1},{1,0},{2,3},{3,2},{4,5},{5,4},{6,7},{7,6},{8,9},{9,8},{10,11... | collective-permute-start | bytes 393224 | tf_op jit(solution)/shard_map/ppermute | solution.py:310
  52.4 3.0 %collective-permute-start.15 = (f32[32,512]{1,0:T(8,128)S(1)}, f32[32,512]{1,0:T(8,128)S(1)}, u32[]{:S(2)}, u32[]{:S(2)}) collective-permute-start(f32[32,512]{1,0:T(8,128)S(1)} %get-tuple-element.20), channel_id=1, source_target_pairs={{0,16},{1,17},{2,18},{3,19},{4,20},{5,21},{6,22},{7,23},{8,24},{9,... | collective-permute-start | bytes 196616 | tf_op jit(solution)/shard_map/ppermute | solution.py:310
  55.5 0.0 collective-permute-done.13.value
  55.5 0.0 collective-permute-start.14
  55.5 2.4 %collective-permute-done.15.last = f32[32,512]{1,0:T(8,128)S(1)} collective-permute-done((f32[32,512]{1,0:T(8,128)S(1)}, f32[32,512]{1,0:T(8,128)S(1)}, u32[]{:S(2)}, u32[]{:S(2)}) %collective-permute-start.15) | collective-permute-done | bytes 65568 | tf_op jit(solution)/shard_map/ppermute | solution.py:310
  57.9 0.0 collective-permute-done.12.refs_5_.kept_other
  57.9 0.9 %shard_map.101.token.lower = f32[96,256]{1,0:T(8,128)S(1)} custom-call(s32[1,2,4]{2,1,0:T(2,128)S(1)} %bitcast.7, f32[64,256]{1,0:T(8,128)S(1)} %shard_map.92.own.token.leaf_own, f32[64,256]{1,0:T(8,128)S(1)} %collective-permute-done.2.sibling.leaf_sibling, f32[32,1024]{1,0:T(8,128)S(1)} %get-tuple-element.17.refs_0_, ...), custom_call_target="tpu_custom_call" | custom-call | flops 10000000000 | bytes 1048576 | tf_op jit(solution)/shard_map/pallas_call | solution.py:379
  58.8 0.0 copy-start.7
  58.8 0.1 collective-permute-start.16
  58.9 3.4 %shard_map.103.near_field = f32[32,1024]{1,0:T(8,128)S(1)} custom-call(s32[1,7]{1,0:T(1,128)S(1)} %copy-done.9, f32[32,1024]{1,0:T(8,128)S(1)} %shard_map.99.token.near_in, bf16[208,1024]{1,0:T(8,128)(2,1)S(1)} %get-tuple-element.14.features, f32[96,256]{1,0:T(8,128)S(1)} %shard_map.101.token.lower, f32[128,1024]{1,0:T(8,128)S(1)} %shard_map.102.refs_0_, ...), custom_call_target="tpu_custom_call" | custom-call | flops 40000000000 | bytes 1048576 | tf_op jit(solution)/shard_map/pallas_call | solution.py:319
  62.3 2.2 %shard_map.105 = f32[32,1024]{1,0:T(8,128)} custom-call(s32[1,2,4]{2,1,0:T(2,128)S(1)} %bitcast.8, f32[1,32]{1,0:T(1,128)S(1)} %bitcast.9, f32[128,1024]{1,0:T(8,128)S(1)} %shard_map.91.chip, f32[1,256,1024]{2,1,0:T(8,128)S(1)} %copy-done.2, f32[1,3,256,512]{3,2,1,0:T(8,128)S(1)} %copy-done, f32[32,1024]{1,0:T(8,128)S(1)} %shard_map.103.near_field, ...), custom_call_target="tpu_custom_call" | custom-call | flops 1000000000 | bytes 1048576 | tf_op jit(solution)/shard_map/pallas_call | solution.py:385
  (22 shorter events, 0.1 us)
Async XLA Ops:
  0.0 1.6 %collective-permute-start = (f32[32,1024]{1,0:T(8,128)}, f32[32,1024]{1,0:T(8,128)S(1)}, u32[]{:S(2)}, u32[]{:S(2)}) collective-permute-start(f32[32,1024]{1,0:T(8,128)} %points.1), channel_id=1, source_target_pairs={{0,1},{1,0},{2,3},{3,2},{4,5},{5,4},{6,7},{7,6},{8,9},{9,8},{10,11... | collective-permute-start | bytes 393224 | tf_op jit(solution)/shard_map/ppermute | solution.py:310
  0.0 1.7 %collective-permute-start.1 = (f32[32,1024]{1,0:T(8,128)}, f32[32,1024]{1,0:T(8,128)S(1)}, u32[]{:S(2)}, u32[]{:S(2)}) collective-permute-start(f32[32,1024]{1,0:T(8,128)} %charges.1), channel_id=1, source_target_pairs={{0,1},{1,0},{2,3},{3,2},{4,5},{5,4},{6,7},{7,6},{8,9},{9,8},{10,11... | collective-permute-start | bytes 393224 | tf_op jit(solution)/shard_map/ppermute | solution.py:310
  1.7 0.9 %copy-start.3 = (f32[32,1024]{1,0:T(8,128)S(1)}, f32[32,1024]{1,0:T(8,128)}, u32[]{:S(2)}) copy-start(f32[32,1024]{1,0:T(8,128)} %points.1) | copy-start | bytes 393220
  2.7 0.9 %copy-start.4 = (f32[32,1024]{1,0:T(8,128)S(1)}, f32[32,1024]{1,0:T(8,128)}, u32[]{:S(2)}) copy-start(f32[32,1024]{1,0:T(8,128)} %charges.1) | copy-start | bytes 393220
  3.6 16.9 %copy-start.5 = (s32[1,3,256]{2,0,1:T(1,128)S(1)}, s32[1,3,256]{2,0,1:T(1,128)}, u32[]{:S(2)}) copy-start(s32[1,3,256]{2,0,1:T(1,128)} %param.12) | copy-start | bytes 9220
  3.6 16.9 %copy-start = (f32[1,3,256,512]{3,2,1,0:T(8,128)S(1)}, f32[1,3,256,512]{3,2,1,0:T(8,128)}, u32[]{:S(2)}) copy-start(f32[1,3,256,512]{3,2,1,0:T(8,128)} %upper_matrix.1) | copy-start | bytes 4718596
  3.6 19.8 %collective-permute-start.4 = (f32[128,1024]{1,0:T(8,128)S(1)}, f32[128,1024]{1,0:T(8,128)S(1)}, u32[]{:S(2)}, u32[]{:S(2)}) collective-permute-start(f32[128,1024]{1,0:T(8,128)S(1)} %shard_map.91.chip), channel_id=1, source_target_pairs={{0,4},{2,6},{4,8},{5,1},{6,10},{7,3},{8,12},{9,5},{10,14},{11,7},{... | collective-permute-start | bytes 1572872 | tf_op jit(solution)/shard_map/ppermute | solution.py:315
  8.9 23.3 %collective-permute-start.7 = (f32[128,1024]{1,0:T(8,128)S(1)}, f32[128,1024]{1,0:T(8,128)S(1)}, u32[]{:S(2)}, u32[]{:S(2)}) collective-permute-start(f32[128,1024]{1,0:T(8,128)S(1)} %shard_map.91.chip), channel_id=1, source_target_pairs={{0,2},{2,4},{3,1},{4,6},{5,3},{6,8},{7,5},{8,10},{9,7},{10,12},{11... | collective-permute-start | bytes 1572872 | tf_op jit(solution)/shard_map/ppermute | solution.py:315
  12.8 1.2 %copy-start.1 = (f32[1,256,1024]{2,1,0:T(8,128)S(1)}, f32[1,256,1024]{2,1,0:T(8,128)}, u32[]{:S(2)}) copy-start(f32[1,256,1024]{2,1,0:T(8,128)} %leaf_matrix.1) | copy-start | bytes 3145732
  14.0 0.7 %copy-start.8 = (s32[1,256]{1,0:T(1,128)S(1)}, s32[1,256]{1,0:T(1,128)}, u32[]{:S(2)}) copy-start(s32[1,256]{1,0:T(1,128)} %chosen.1) | copy-start | bytes 3076
  15.2 6.5 %copy-start.9 = (s32[1,7]{1,0:T(1,128)S(1)}, s32[1,7]{1,0:T(1,128)}, u32[]{:S(2)}) copy-start(s32[1,7]{1,0:T(1,128)} %near.5) | copy-start | bytes 88
  15.2 5.2 %collective-permute-start.2 = (f32[64,256]{1,0:T(8,128)S(1)}, f32[64,256]{1,0:T(8,128)S(1)}, u32[]{:S(2)}, u32[]{:S(2)}) collective-permute-start(f32[64,256]{1,0:T(8,128)S(1)} %shard_map.92.own.token.leaf_own), channel_id=1, source_target_pairs={{0,1},{1,0},{2,3},{3,2},{4,5},{5,4},{6,7},{7,6},{8,9},{9,8},{10,11... | collective-permute-start | bytes 196616 | tf_op jit(solution)/shard_map/ppermute | solution.py:310
  20.6 8.4 %collective-permute-start.3 = (f32[32,768]{1,0:T(8,128)S(1)}, f32[32,768]{1,0:T(8,128)S(1)}, u32[]{:S(2)}, u32[]{:S(2)}) collective-permute-start(f32[32,768]{1,0:T(8,128)S(1)} %shard_map.93.token.own), channel_id=1, source_target_pairs={{0,2},{1,3},{2,0},{3,1},{4,6},{5,7},{6,4},{7,5},{8,10},{9,11},{10,... | collective-permute-start | bytes 294920 | tf_op jit(solution)/shard_map/ppermute | solution.py:310
  32.3 11.2 %collective-permute-start.8 = (f32[128,1024]{1,0:T(8,128)S(1)}, f32[128,1024]{1,0:T(8,128)S(1)}, u32[]{:S(2)}, u32[]{:S(2)}) collective-permute-start(f32[128,1024]{1,0:T(8,128)S(1)} %shard_map.98.refs_2_), channel_id=1, source_target_pairs={{0,1},{1,0},{2,3},{3,2},{4,5},{5,4},{6,7},{7,6},{8,9},{9,8},{10,11... | collective-permute-start | bytes 1572872 | tf_op jit(solution)/shard_map/ppermute | solution.py:310
  33.2 10.4 %collective-permute-start.6 = (f32[128,1024]{1,0:T(8,128)S(1)}, f32[128,1024]{1,0:T(8,128)S(1)}, u32[]{:S(2)}, u32[]{:S(2)}) collective-permute-start(f32[128,1024]{1,0:T(8,128)S(1)} %shard_map.95.token.refs_0_), channel_id=1, source_target_pairs={{0,1},{1,0},{2,3},{3,2},{4,5},{5,4},{6,7},{7,6},{8,9},{9,8},{10,11... | collective-permute-start | bytes 1572872 | tf_op jit(solution)/shard_map/ppermute | solution.py:310
  33.3 8.1 %collective-permute-start.5 = (f32[32,768]{1,0:T(8,128)S(1)}, f32[32,768]{1,0:T(8,128)S(1)}, u32[]{:S(2)}, u32[]{:S(2)}) collective-permute-start(f32[32,768]{1,0:T(8,128)S(1)} %get-tuple-element.15.own.token), channel_id=1, source_target_pairs={{0,4},{1,5},{2,6},{3,7},{4,0},{5,1},{6,2},{7,3},{8,12},{9,13},{10,... | collective-permute-start | bytes 294920 | tf_op jit(solution)/shard_map/ppermute | solution.py:310
  34.2 21.3 %collective-permute-start.13 = (f32[128,1024]{1,0:T(8,128)S(1)}, f32[128,1024]{1,0:T(8,128)S(1)}, u32[]{:S(2)}, u32[]{:S(2)}) collective-permute-start(f32[128,1024]{1,0:T(8,128)S(1)} %shard_map.95.token.refs_0_), channel_id=1, source_target_pairs={{0,2},{2,4},{3,1},{4,6},{5,3},{6,8},{7,5},{8,10},{9,7},{10,12},{11... | collective-permute-start | bytes 1572872 | tf_op jit(solution)/shard_map/ppermute | solution.py:315
  38.5 19.3 %collective-permute-start.9 = (f32[32,1024]{1,0:T(8,128)S(1)}, f32[32,1024]{1,0:T(8,128)S(1)}, u32[]{:S(2)}, u32[]{:S(2)}) collective-permute-start(f32[32,1024]{1,0:T(8,128)S(1)} %get-tuple-element.17.refs_0_), channel_id=1, source_target_pairs={{0,1},{1,0},{2,3},{3,2},{4,5},{5,4},{6,7},{7,6},{8,9},{9,8},{10,11... | collective-permute-start | bytes 393224 | tf_op jit(solution)/shard_map/ppermute | solution.py:310
  41.5 9.4 %collective-permute-start.11 = (f32[32,768]{1,0:T(8,128)S(1)}, f32[32,768]{1,0:T(8,128)S(1)}, u32[]{:S(2)}, u32[]{:S(2)}) collective-permute-start(f32[32,768]{1,0:T(8,128)S(1)} %get-tuple-element.16.token.own), channel_id=1, source_target_pairs={{0,8},{1,9},{2,10},{3,11},{4,12},{5,13},{6,14},{7,15},{8,0},{9,1},... | collective-permute-start | bytes 294920 | tf_op jit(solution)/shard_map/ppermute | solution.py:310
  43.5 14.3 %collective-permute-start.10 = (f32[32,1024]{1,0:T(8,128)S(1)}, f32[32,1024]{1,0:T(8,128)S(1)}, u32[]{:S(2)}, u32[]{:S(2)}) collective-permute-start(f32[32,1024]{1,0:T(8,128)S(1)} %get-tuple-element.18.refs_2_), channel_id=1, source_target_pairs={{0,1},{1,0},{2,3},{3,2},{4,5},{5,4},{6,7},{7,6},{8,9},{9,8},{10,11... | collective-permute-start | bytes 393224 | tf_op jit(solution)/shard_map/ppermute | solution.py:310
  50.1 7.8 %copy-start.6 = (s32[1,4,2]{1,2,0:T(2,128)S(1)}, s32[1,4,2]{1,2,0:T(2,128)}, u32[]{:S(2)}) copy-start(s32[1,4,2]{1,2,0:T(2,128)} %param.16) | copy-start | bytes 100
  50.9 6.9 %collective-permute-start.12 = (f32[32,1024]{1,0:T(8,128)S(1)}, f32[32,1024]{1,0:T(8,128)S(1)}, u32[]{:S(2)}, u32[]{:S(2)}) collective-permute-start(f32[32,1024]{1,0:T(8,128)S(1)} %get-tuple-element.19.refs_4_.kept), channel_id=1, source_target_pairs={{0,1},{1,0},{2,3},{3,2},{4,5},{5,4},{6,7},{7,6},{8,9},{9,8},{10,11... | collective-permute-start | bytes 393224 | tf_op jit(solution)/shard_map/ppermute | solution.py:310
  52.4 5.4 %collective-permute-start.15 = (f32[32,512]{1,0:T(8,128)S(1)}, f32[32,512]{1,0:T(8,128)S(1)}, u32[]{:S(2)}, u32[]{:S(2)}) collective-permute-start(f32[32,512]{1,0:T(8,128)S(1)} %get-tuple-element.20), channel_id=1, source_target_pairs={{0,16},{1,17},{2,18},{3,19},{4,20},{5,21},{6,22},{7,23},{8,24},{9,... | collective-permute-start | bytes 196616 | tf_op jit(solution)/shard_map/ppermute | solution.py:310
  55.5 3.4 %collective-permute-start.14 = (f32[128,1024]{1,0:T(8,128)S(1)}, f32[128,1024]{1,0:T(8,128)S(1)}, u32[]{:S(2)}, u32[]{:S(2)}) collective-permute-start(f32[128,1024]{1,0:T(8,128)S(1)} %shard_map.102.refs_0_), channel_id=1, source_target_pairs={{0,1},{1,0},{2,3},{3,2},{4,5},{5,4},{6,7},{7,6},{8,9},{9,8},{10,11... | collective-permute-start | bytes 1572872 | tf_op jit(solution)/shard_map/ppermute | solution.py:310
  58.8 3.5 %copy-start.2 = (f32[1,256,1024]{2,1,0:T(8,128)S(1)}, f32[1,256,1024]{2,1,0:T(8,128)}, u32[]{:S(2)}) copy-start(f32[1,256,1024]{2,1,0:T(8,128)} %leaf_matrix.1) | copy-start | bytes 3145732
  58.8 3.5 %copy-start.7 = (f32[32]{0:T(128)S(1)}, f32[32]{0:T(128)}, u32[]{:S(2)}) copy-start(f32[32]{0:T(128)} %param.17) | copy-start | bytes 388
  58.8 3.5 %collective-permute-start.16 = (f32[32,512]{1,0:T(8,128)S(1)}, f32[32,512]{1,0:T(8,128)S(1)}, u32[]{:S(2)}, u32[]{:S(2)}) collective-permute-start(f32[32,512]{1,0:T(8,128)S(1)} %shard_map.104), channel_id=1, source_target_pairs={{0,1},{1,0},{2,3},{3,2},{4,5},{5,4},{6,7},{7,6},{8,9},{9,8},{10,11... | collective-permute-start | bytes 196616 | tf_op jit(solution)/shard_map/ppermute | solution.py:310

commit v2 on v1

--- a/solution.py
+++ b/solution.py
@@ -146,7 +146,11 @@
     near_out[...] = near_in[...] + sum3(total[...])
 
 
-def merge(level, own, sibling, chosen, matrix, token, sent, extra=None):
+def block_of(ref, place):
+    return ref[:, RANK * place : RANK * (place + 1)]
+
+
+def merge(level, own, sibling, chosen, matrix, token, sent, *more):
     me = lax.axis_index("leaf")
     right = lax.rem(lax.shift_right_logical(me, level), 2)
     kind = lax.rem(me, 2)
@@ -155,15 +159,14 @@
         mine = own[rows, :]
         theirs = sibling[rows, :]
     else:
-        mine = own[:, 2 * RANK :]
-        theirs = sibling[:, 2 * RANK :]
-        extra[:, : 2 * RANK] = sibling[:, : 2 * RANK]
-        extra[:, 2 * RANK : 3 * RANK] = mine
-        extra[:, 3 * RANK :] = theirs
+        mine = block_of(own, 2)
+        theirs = block_of(sibling, 2)
+        kept = more[-1]
+        kept[:, : 2 * RANK] = sibling[:, : 2 * RANK]
+        kept[:, 2 * RANK : 3 * RANK] = mine
+        kept[:, 3 * RANK : 4 * RANK] = theirs
     sent[:, :RANK] = mine
     sent[:, RANK : 2 * RANK] = theirs
-    if level == LEVELS - 1:
-        return
     mine = stack3(mine)
     theirs = stack3(theirs)
     first = right * RANK
@@ -172,9 +175,8 @@
     @pl.when(kind == 0)
     def _():
         spots = lax.broadcasted_iota(jnp.int32, (RANK, RANK), 0)
-        row = chosen[level]
-        left_marks = (spots + first == row).astype(f32).astype(bf16)
-        right_marks = (spots + second == row).astype(f32).astype(bf16)
+        left_marks = (spots + first == chosen[level]).astype(f32).astype(bf16)
+        right_marks = (spots + second == chosen[level]).astype(f32).astype(bf16)
         sent[:, 2 * RANK :] = sum3(mm(mine, left_marks) + mm(theirs, right_marks))
 
     @pl.when(kind == 1)
@@ -190,11 +192,21 @@
             + (mm(theirs, far_high, NT) + mm(theirs, far_low, NT))
         )
 
+    if level == 2:
+        more[0][...] = block_of(sent, 2)
+        kept[:, 4 * RANK :] = block_of(sent, 2)
+
+
+def collect(far_one, far_two, far_three, token, out):
+    out[:, : 3 * RANK] = far_one[...]
+    out[:, 3 * RANK : 4 * RANK] = far_two[...]
+    out[:, 4 * RANK :] = far_three[...]
+
 
 def sorted_kinds(pair, mine, theirs):
     kind = lax.rem(lax.axis_index("leaf"), 2)
-    left = pair[0][:, RANK * mine : RANK * (mine + 1)]
-    right = pair[1][:, RANK * theirs : RANK * (theirs + 1)]
+    left = block_of(pair[0], mine)
+    right = block_of(pair[1], theirs)
     return jnp.where(kind == 0, left, right), jnp.where(kind == 0, right, left)
 
 
@@ -214,49 +226,55 @@
     return sum3(mm(weights, high) + mm(weights, low))
 
 
-def far_lower(codes, leaf_own, leaf_sibling, *refs):
-    kept = [refs[0:2], refs[2:4], refs[4:6]]
-    out = refs[6]
+def product(left, right):
+    high, low = split2(right)
+    pieces = stack3(left)
+    return sum3(mm(pieces, high) + mm(pieces, low))
+
+
+def half_of(matrix, level):
+    right = lax.rem(lax.shift_right_logical(lax.axis_index("leaf"), level), 2)
+    return matrix[0, level, :, pl.ds(pl.multiple_of(right * RANK, RANK), RANK)]
+
+
+def compose(upper_matrix, leaf_matrix, token, out):
+    value = leaf_matrix[0]
+    for level in range(3):
+        value = product(half_of(upper_matrix, level), value)
+        out[level] = value
+
+
+def far_first(
+    codes, gain, mine, leaf_matrix, composed, leaf_own, leaf_sibling, low, low_other, middle, middle_other, token, out
+):
+    low = (low, low_other)
+    middle = (middle, middle_other)
     choices = [
         (leaf_sibling[:32], leaf_sibling[32:]),
-        sorted_kinds(kept[0], 0, 1),
-        sorted_kinds(kept[0], 1, 0),
+        sorted_kinds(low, 0, 1),
+        sorted_kinds(low, 1, 0),
     ]
-    out[:32] = far_level(0, codes, leaf_own[:32], choices)
-    for level in (1, 2):
-        choices = [
-            sorted_kinds(kept[level - 1], 3, 3),
-            sorted_kinds(kept[level], 0, 0),
-            sorted_kinds(kept[level], 1, 1),
-        ]
-        own = sorted_kinds(kept[level - 1], 2, 2)[0]
-        out[32 * level : 32 * level + 32] = far_level(level, codes, own, choices)
-
-
-def finish(
-    codes, gain, chip, leaf_matrix, upper_matrix, near_field, lower, kept, kept_other, last, last_other, out
-):
-    me = lax.axis_index("leaf")
+    first = far_level(0, codes, leaf_own[:32], choices)
+    choices = [sorted_kinds(low, 3, 3), sorted_kinds(middle, 0, 0), sorted_kinds(middle, 1, 1)]
+    second = far_level(1, codes, sorted_kinds(low, 2, 2)[0], choices)
+    count = gain.shape[1]
+    diagonal = lax.broadcasted_iota(jnp.int32, (count, count), 0) == lax.broadcasted_iota(
+        jnp.int32, (count, count), 1
+    )
+    column = jnp.sum(jnp.where(diagonal, gain[...], 0.0), axis=1, keepdims=True)
+    far_out = product(first, leaf_matrix[0]) + product(second, composed[0])
+    out[...] = far_out + column * mine[32:64]
+
+
+def finish(codes, composed, near_field, lower, kept, kept_other, last, last_other, out):
     kept = (kept, kept_other)
     last = (last, last_other)
     choices = [sorted_kinds(kept, 3, 3), sorted_kinds(last, 0, 0), sorted_kinds(last, 1, 1)]
-    local = far_level(3, codes, sorted_kinds(kept, 2, 2)[0], choices)
-    for level in reversed(range(LEVELS - 1)):
-        right = lax.rem(lax.shift_right_logical(me, level), 2)
-        columns = pl.ds(pl.multiple_of(right * RANK, RANK), RANK)
-        half = upper_matrix[0, level, :, columns]
-        high, low = split2(half)
-        pieces = stack3(local)
-        local = lower[32 * level : 32 * level + 32] + sum3(mm(pieces, high) + mm(pieces, low))
-    high, low = split2(leaf_matrix[0])
-    pieces = stack3(local)
-    far_out = sum3(mm(pieces, high) + mm(pieces, low))
-    count = gain.shape[1]
-    diagonal = lax.broadcasted_iota(jnp.int32, (count, count), 0) == lax.broadcasted_iota(
-        jnp.int32, (count, count), 1
-    )
-    column = jnp.sum(jnp.where(diagonal, gain[...], 0.0), axis=1, keepdims=True)
-    out[...] = far_out + near_field[...] + column * chip[32:64]
+    third = far_level(2, codes, sorted_kinds(kept, 2, 2)[0], choices)
+    choices = [sorted_kinds(last, place, place) for place in (2, 3, 4)]
+    fourth = far_level(3, codes, sorted_kinds(kept, 4, 4)[0], choices)
+    far_out = product(third, composed[1]) + product(fourth, composed[2])
+    out[...] = (far_out + lower[...]) + near_field[...]
 
 
 def call(function, shapes, in_specs, flops, scratch=(), limit=16, **extra):
@@ -275,6 +293,16 @@
 
 def gate(value, token, out):
     pass
+
+
+def halve(value, token, whole, upper, lower):
+    whole[...] = value[...]
+    upper[...] = value[:64]
+    lower[...] = value[64:]
+
+
+def second_half(value, token, out):
+    out[...] = value[64:]
 
 
 def after(value, token):
@@ -307,20 +335,20 @@
     size = points.shape[1]
 
     def partner(value, bit):
-        return lax.ppermute(value, "leaf", [(leaf, leaf ^ (1 << bit)) for leaf in range(devices)])
+        return lax.ppermute(value, "leaf", [(leaf, leaf ^ bit) for leaf in range(devices)])
 
     def along(value, chips):
         pairs = [(leaf, leaf + 2 * chips * (1 - 2 * (leaf % 2))) for leaf in range(devices)]
         pairs = [(source, target) for source, target in pairs if 0 <= target < devices]
         return lax.ppermute(value, "leaf", pairs)
 
-    def near_step(near_field, token, sources, entries):
+    def near_step(near_field, token, sources, entries, flops):
         count = len(sources)
         return call(
             functools.partial(near_blocks, entries, count),
             shape(32, size),
             [VMEM] * 3 + [ANY] * (1 + count),
-            4 * 10**10,
+            flops,
             [
                 pltpu.VMEM((len(entries), 64, size), f32),
                 pltpu.VMEM((96, size), f32),
@@ -329,9 +357,11 @@
         )(near_leaves, near_field, features, token, *sources)
 
     def merge_step(level, own, sibling, token):
-        shapes = [shape(32, (3 if level < LEVELS - 1 else 2) * RANK)]
-        if level > 0:
-            shapes.append(shape(32, 4 * RANK))
+        shapes = [shape(32, 3 * RANK)]
+        if level == 1:
+            shapes += [shape(32, 4 * RANK)]
+        if level == 2:
+            shapes += [shape(32, RANK), shape(32, 5 * RANK)]
         return call(functools.partial(merge, level), shapes, [VMEM] * 4 + [ANY], 10**8)(
             own, sibling, upper_chosen, upper_projection, token
         )
@@ -340,60 +370,74 @@
     codes = jnp.transpose(far_codes, (0, 2, 1))
 
     chip = call(pair, shape(128, size), [VMEM] * 4, 10**8)(
-        points, charges, partner(points, 0), partner(charges, 0)
+        points, charges, partner(points, 1), partner(charges, 1)
     )
     got2 = along(chip, 2)
     got1 = along(chip, 1)
     node = call(leaf_node, shape(64, RANK), [VMEM] * 3, 10**11)(
         chip, leaf_skeleton, leaf_projection
     )
-    sibling_node = partner(node, 0)
+    sibling_node = partner(node, 1)
     (sent1,) = merge_step(0, node, sibling_node, node)
-    far1 = partner(sent1, 1)
+    far1 = partner(sent1, 2)
     near_field, features = call(
         near_first,
         [shape(32, size), shape(208, size, bf16)],
         [VMEM] * 2 + [ANY],
-        2 * 10**9,
+        10**5,
         [pltpu.VMEM((96, size), f32)],
     )(near_leaves, chip, sent1)
-    got2 = after(got2, near_field)
-    sent2, kept2 = merge_step(1, sent1, far1, got2)
-    far2 = partner(sent2, 2)
-    kept2_other = partner(kept2, 0)
+    composed = call(
+        compose,
+        jax.ShapeDtypeStruct((3, RANK, size), f32),
+        [VMEM, VMEM, ANY],
+        10**5,
+    )(upper_projection, leaf_projection, near_field)
+    got2, upper2, lower2 = call(
+        halve, [shape(128, size), shape(64, size), shape(64, size)], [VMEM, ANY], 10**5
+    )(got2, composed)
+    sources = [got2, partner(upper2, 1), partner(lower2, 1)]
+    entries = [(0, 0, 4), (0, 64, 3), (1, 0, -5), (2, 0, -4)]
+    near_field = near_step(near_field, composed, sources, entries, 10**5)
+    sent2, kept2 = merge_step(1, sent1, far1, near_field)
+    far2 = partner(sent2, 4)
+    kept2_other = partner(kept2, 1)
+    got1 = after(got1, sent2)
     got3 = along(got2, 1)
-    other2 = partner(got2, 0)
-    sent3, kept3 = merge_step(2, sent2, far2, near_field)
-    far3 = partner(sent3, 3)
-    kept3_other = partner(kept3, 0)
-    got1 = after(got1, sent2)
-    other1 = partner(got1, 0)
-    entries = [(0, 0, 4), (0, 64, 3), (1, 0, -5), (1, 64, -4)]
-    entries += [(2, 0, 2), (2, 64, 1), (3, 0, -3), (3, 64, -2)]
-    near_field = near_step(near_field, sent3, [got2, other2, got1, other1], entries)
-    sent4, kept4 = merge_step(3, sent3, far3, near_field)
-    far4 = partner(sent4, 4)
-    kept4_other = partner(kept4, 0)
-    got3 = after(got3, near_field)
-    other3 = partner(got3, 0)
-    lower = call(far_lower, shape(96, RANK), [VMEM] * 9, 10**10)(
-        codes, node, sibling_node, kept2, kept2_other, kept3, kept3_other, kept4, kept4_other
-    )
-    far4_other = partner(after(far4, lower), 0)
-    entries = [(0, 0, 6), (0, 64, 5), (1, 64, -6)]
-    near_field = near_step(near_field, lower, [got3, other3], entries)
-    return call(finish, shape(32, size), [VMEM] * 11, 10**9)(
+    other1 = partner(got1, 1)
+    sent3, sent_few, kept3 = merge_step(2, sent2, far2, near_field)
+    far_one = partner(sent3, 8)
+    far_two = partner(sent_few, 16)
+    far_three = partner(sent_few, 24)
+    kept3_other = partner(kept3, 1)
+    entries = [(0, 0, 2), (0, 64, 1), (1, 0, -3), (1, 64, -2)]
+    near_field = near_step(near_field, sent3, [got1, other1], entries, 4 * 10**10)
+    lower = call(far_first, shape(32, size), [VMEM] * 11 + [ANY], 10**8)(
         codes,
         regularizer[None, :],
         chip,
         leaf_projection,
-        upper_projection,
+        composed,
+        node,
+        sibling_node,
+        kept2,
+        kept2_other,
+        kept3,
+        kept3_other,
         near_field,
-        lower,
-        kept4,
-        kept4_other,
-        far4,
-        far4_other,
+    )
+    got3 = after(got3, lower)
+    near_field = near_step(near_field, lower, [got3], [(0, 0, 6), (0, 64, 5)], 10**5)
+    last = call(collect, shape(32, 5 * RANK), [VMEM] * 3 + [ANY], 10**8)(
+        far_one, far_two, far_three, near_field
+    )
+    last_other = partner(last, 1)
+    other3 = partner(
+        call(second_half, shape(64, size), [VMEM, ANY], 10**5)(got3, last), 1
+    )
+    near_field = near_step(near_field, last, [other3], [(0, 0, -6)], 10**10)
+    return call(finish, shape(32, size), [VMEM] * 8, 10**9)(
+        codes, composed, near_field, lower, kept3, kept3_other, last, last_other
     )
 
 

time: 65.1 us -> 64 us (0.983)
  waiting for transfers between devices: 14.8 us -> 9.25 us
  Pallas kernels: 15.6 us -> 18.6 us
  starting transfers between devices: 30.1 us -> 31.8 us
    ppermute x3, waiting for transfers between devices: 3.25 us -> 0.04 us  [along(): return lax.ppermute(value, 'leaf', pairs)]
    pallas_call x2 -> x6, Pallas kernels: 3.06 us -> 5.7 us  [the longest x1 2.64 us: body(): call(compose, jax.ShapeDtypeStruct((3, RANK, size), f32), [VMEM, VMEM, AN...]
    ppermute x14 -> x15, waiting for transfers between devices: 11.5 us -> 9.21 us  [partner(): lax.ppermute(value, 'leaf', [(leaf, leaf ^ bit) for leaf in range(devices)])]
    ppermute x14 -> x15, starting transfers between devices: 16.6 us -> 18.3 us  [partner(): lax.ppermute(value, 'leaf', [(leaf, leaf ^ bit) for leaf in range(devices)])]
    pallas_call x2 -> x4, Pallas kernels: 9.91 us -> 10.3 us  [near_step(): call(functools.partial(near_blocks, entries, count), shape(32, size), [VM...]
    unnamed x21 -> x20, local copies, waits for them, and re-layouts: 3.79 us -> 3.79 us
  transfers between devices with their start and end apart: 17 -> 18, of which waited for: 9 -> 6; matrix products, arithmetic and copies ran while one was open for 0% -> 0% of each run, Pallas kernels for 21% -> 26%
where the time goes in v2:
time: 64 us; the launch traced here: 63.8 us
  starting transfers between devices  31.8 us (50%)
  Pallas kernels  18.6 us (29%)
  waiting for transfers between devices  9.25 us (14%)
  local copies, waits for them, and re-layouts  3.79 us (6%)
    ppermute x15, starting transfers between devices, partner(): lax.ppermute(value, 'leaf', [(leaf, leaf ^ bit) for leaf in range(devices)])  18.3 us
    ppermute x3, starting transfers between devices, along(): return lax.ppermute(value, 'leaf', pairs)  13.5 us
    pallas_call x4, Pallas kernels, near_step(): call(functools.partial(near_blocks, entries, count), shape(32, size), [VM...  10.3 us
    ppermute x15, waiting for transfers between devices, partner(): lax.ppermute(value, 'leaf', [(leaf, leaf ^ bit) for leaf in range(devices)])  9.21 us
    unnamed x20, local copies, waits for them, and re-layouts  3.79 us
    pallas_call x1, Pallas kernels, body(): call(compose, jax.ShapeDtypeStruct((3, RANK, size), f32), [VMEM, VMEM, AN...  2.64 us
    pallas_call x1, Pallas kernels, body(): call(finish, shape(32, size), [VMEM] * 8, 10 ** 9)  1.88 us
    pallas_call x1, Pallas kernels, body(): call(near_first, [shape(32, size), shape(208, size, bf16)], [VMEM] * 2 +...  1.54 us
  transfers between devices with their start and end apart: 18, of which 6 were waited for; matrix products, arithmetic and copies ran while one was open for 0% of the time, Pallas kernels for 26%

profile of v2, /device:TPU:24, one launch (start us, length us, event | category | flops | bytes accessed | tf_op | source)
XLA Modules:
  0.0 63.8 jit_solution(16087947838891413801)
XLA Ops:
  0.0 0.5 collective-permute-start.1
  0.5 1.0 %collective-permute-done.other_points = f32[32,1024]{1,0:T(8,128)S(1)} collective-permute-done((f32[32,1024]{1,0:T(8,128)}, f32[32,1024]{1,0:T(8,128)S(1)}, u32[]{:S(2)}, u32[]{:S(2)}) %collective-permute-start) | collective-permute-done | bytes 131104 | tf_op jit(solution)/shard_map/ppermute | solution.py:338
  1.6 0.2 collective-permute-done.1.other_charges
  1.7 0.9 %copy-done.3 = f32[32,1024]{1,0:T(8,128)S(1)} copy-done((f32[32,1024]{1,0:T(8,128)S(1)}, f32[32,1024]{1,0:T(8,128)}, u32[]{:S(2)}) %copy-start.3) | copy-done | bytes 131096
  2.7 0.9 %copy-done.4 = f32[32,1024]{1,0:T(8,128)S(1)} copy-done((f32[32,1024]{1,0:T(8,128)S(1)}, f32[32,1024]{1,0:T(8,128)}, u32[]{:S(2)}) %copy-start.4) | copy-done | bytes 131096
  3.6 0.0 copy-start
  3.6 5.3 %collective-permute-start.3 = (f32[128,1024]{1,0:T(8,128)S(1)}, f32[128,1024]{1,0:T(8,128)S(1)}, u32[]{:S(2)}, u32[]{:S(2)}) collective-permute-start(f32[128,1024]{1,0:T(8,128)S(1)} %shard_map.91.chip.mine), channel_id=1, source_target_pairs={{0,4},{2,6},{4,8},{5,1},{6,10},{7,3},{8,12},{9,5},{10,14},{11,7},{... | collective-permute-start | bytes 1572872 | tf_op jit(solution)/shard_map/ppermute | solution.py:343
  8.9 3.8 %collective-permute-start.8 = (f32[128,1024]{1,0:T(8,128)S(1)}, f32[128,1024]{1,0:T(8,128)S(1)}, u32[]{:S(2)}, u32[]{:S(2)}) collective-permute-start(f32[128,1024]{1,0:T(8,128)S(1)} %shard_map.91.chip.mine), channel_id=1, source_target_pairs={{0,2},{2,4},{3,1},{4,6},{5,3},{6,8},{7,5},{8,10},{9,7},{10,12},{11... | collective-permute-start | bytes 1572872 | tf_op jit(solution)/shard_map/ppermute | solution.py:343
  12.8 0.0 copy-start.1
  12.8 1.2 %copy-done.1 = f32[1,256,1024]{2,1,0:T(8,128)S(1)} copy-done((f32[1,256,1024]{2,1,0:T(8,128)S(1)}, f32[1,256,1024]{2,1,0:T(8,128)}, u32[]{:S(2)}) %copy-start.1) | copy-done | bytes 1048600
  14.0 0.7 %copy-done.9 = s32[1,256]{1,0:T(1,128)S(1)} copy-done((s32[1,256]{1,0:T(1,128)S(1)}, s32[1,256]{1,0:T(1,128)}, u32[]{:S(2)}) %copy-start.9) | copy-done | bytes 1048
  14.7 0.5 shard_map.92.own.token.leaf_own
  15.2 0.0 copy-start.2
  15.2 4.3 %collective-permute-start.2 = (f32[64,256]{1,0:T(8,128)S(1)}, f32[64,256]{1,0:T(8,128)S(1)}, u32[]{:S(2)}, u32[]{:S(2)}) collective-permute-start(f32[64,256]{1,0:T(8,128)S(1)} %shard_map.92.own.token.leaf_own), channel_id=1, source_target_pairs={{0,1},{1,0},{2,3},{3,2},{4,5},{5,4},{6,7},{7,6},{8,9},{9,8},{10,11... | collective-permute-start | bytes 196616 | tf_op jit(solution)/shard_map/ppermute | solution.py:338
  19.6 0.9 %collective-permute-done.2.sibling.leaf_sibling = f32[64,256]{1,0:T(8,128)S(1)} collective-permute-done((f32[64,256]{1,0:T(8,128)S(1)}, f32[64,256]{1,0:T(8,128)S(1)}, u32[]{:S(2)}, u32[]{:S(2)}) %collective-permute-start.2) | collective-permute-done | bytes 65568 | tf_op jit(solution)/shard_map/ppermute | solution.py:338
  20.5 0.2 shard_map.93.token.own
  20.6 0.0 copy-done.6
  20.7 1.5 %shard_map.94 = (f32[32,1024]{1,0:T(8,128)S(1)}, bf16[208,1024]{1,0:T(8,128)(2,1)S(1)}) custom-call(s32[1,7]{1,0:T(1,128)S(1)} %copy-done.6, f32[128,1024]{1,0:T(8,128)S(1)} %shard_map.91.chip.mine, f32[32,768]{1,0:T(8,128)S(1)} %shard_map.93.token.own), custom_call_target="tpu_custom_call" | custom-call | flops 100000 | bytes 1048576 | tf_op jit(solution)/shard_map/pallas_call | solution.py:383
  22.2 2.6 %shard_map.95.token.composed = f32[3,256,1024]{2,1,0:T(8,128)S(1)} custom-call(f32[1,3,256,512]{3,2,1,0:T(8,128)S(1)} %copy-done, f32[1,256,1024]{2,1,0:T(8,128)S(1)} %copy-done.2, f32[32,1024]{1,0:T(8,128)S(1)} %get-tuple-element.15.token.near_in), custom_call_target="tpu_custom_call" | custom-call | flops 100000 | bytes 1048576 | tf_op jit(solution)/shard_map/pallas_call | solution.py:390
  24.9 0.0 collective-permute-done.3.value
  24.9 0.1 shard_map.96
  25.0 1.3 %collective-permute-start.4 = (f32[64,1024]{1,0:T(8,128)S(1)}, f32[64,1024]{1,0:T(8,128)S(1)}, u32[]{:S(2)}, u32[]{:S(2)}) collective-permute-start(f32[64,1024]{1,0:T(8,128)S(1)} %get-tuple-element.18), channel_id=1, source_target_pairs={{0,1},{1,0},{2,3},{3,2},{4,5},{5,4},{6,7},{7,6},{8,9},{9,8},{10,11... | collective-permute-start | bytes 786440 | tf_op jit(solution)/shard_map/ppermute | solution.py:338
  26.3 0.1 collective-permute-start.5
  26.4 2.5 %collective-permute-start.6 = (f32[32,768]{1,0:T(8,128)S(1)}, f32[32,768]{1,0:T(8,128)S(1)}, u32[]{:S(2)}, u32[]{:S(2)}) collective-permute-start(f32[32,768]{1,0:T(8,128)S(1)} %shard_map.93.token.own), channel_id=1, source_target_pairs={{0,2},{1,3},{2,0},{3,1},{4,6},{5,7},{6,4},{7,5},{8,10},{9,11},{10,... | collective-permute-start | bytes 294920 | tf_op jit(solution)/shard_map/ppermute | solution.py:338
  28.8 1.8 %shard_map.97.token.near_in = f32[32,1024]{1,0:T(8,128)S(1)} custom-call(s32[1,7]{1,0:T(1,128)S(1)} %copy-done.6, f32[32,1024]{1,0:T(8,128)S(1)} %get-tuple-element.15.token.near_in, bf16[208,1024]{1,0:T(8,128)(2,1)S(1)} %get-tuple-element.16.features, f32[3,256,1024]{2,1,0:T(8,128)S(1)} %shard_map.95.token.composed, ...), custom_call_target="tpu_custom_call" | custom-call | flops 100000 | bytes 1048576 | tf_op jit(solution)/shard_map/pallas_call | solution.py:347
  30.7 1.9 %collective-permute-done.6.sibling = f32[32,768]{1,0:T(8,128)S(1)} collective-permute-done((f32[32,768]{1,0:T(8,128)S(1)}, f32[32,768]{1,0:T(8,128)S(1)}, u32[]{:S(2)}, u32[]{:S(2)}) %collective-permute-start.6) | collective-permute-done | bytes 98336 | tf_op jit(solution)/shard_map/ppermute | solution.py:338
  32.6 0.2 shard_map.98
  32.7 0.0 collective-permute-done.8.value
  32.8 1.3 %collective-permute-start.9 = (f32[128,1024]{1,0:T(8,128)S(1)}, f32[128,1024]{1,0:T(8,128)S(1)}, u32[]{:S(2)}, u32[]{:S(2)}) collective-permute-start(f32[128,1024]{1,0:T(8,128)S(1)} %shard_map.100.refs_0_), channel_id=1, source_target_pairs={{0,1},{1,0},{2,3},{3,2},{4,5},{5,4},{6,7},{7,6},{8,9},{9,8},{10,11... | collective-permute-start | bytes 1572872 | tf_op jit(solution)/shard_map/ppermute | solution.py:338
  34.0 0.1 collective-permute-start.10
  34.1 0.1 collective-permute-start.7
  34.2 4.4 %collective-permute-start.12 = (f32[128,1024]{1,0:T(8,128)S(1)}, f32[128,1024]{1,0:T(8,128)S(1)}, u32[]{:S(2)}, u32[]{:S(2)}) collective-permute-start(f32[128,1024]{1,0:T(8,128)S(1)} %get-tuple-element.17.refs_0_), channel_id=1, source_target_pairs={{0,2},{2,4},{3,1},{4,6},{5,3},{6,8},{7,5},{8,10},{9,7},{10,12},{11... | collective-permute-start | bytes 1572872 | tf_op jit(solution)/shard_map/ppermute | solution.py:343
  38.6 4.2 %collective-permute-done.7.sibling = f32[32,768]{1,0:T(8,128)S(1)} collective-permute-done((f32[32,768]{1,0:T(8,128)S(1)}, f32[32,768]{1,0:T(8,128)S(1)}, u32[]{:S(2)}, u32[]{:S(2)}) %collective-permute-start.7) | collective-permute-done | bytes 98336 | tf_op jit(solution)/shard_map/ppermute | solution.py:338
  42.7 0.2 shard_map.99
  43.0 0.1 collective-permute-start.14
  43.1 3.6 %collective-permute-start.15 = (f32[32,256]{1,0:T(8,128)S(1)}, f32[32,256]{1,0:T(8,128)S(1)}, u32[]{:S(2)}, u32[]{:S(2)}) collective-permute-start(f32[32,256]{1,0:T(8,128)S(1)} %get-tuple-element.24), channel_id=1, source_target_pairs={{0,24},{1,25},{2,26},{3,27},{4,28},{5,29},{6,30},{7,31},{8,16},{9,... | collective-permute-start | bytes 98312 | tf_op jit(solution)/shard_map/ppermute | solution.py:338
  46.7 0.0 copy-start.7
  46.7 0.0 copy-start.8
  46.7 3.8 %collective-permute-start.13 = (f32[32,768]{1,0:T(8,128)S(1)}, f32[32,768]{1,0:T(8,128)S(1)}, u32[]{:S(2)}, u32[]{:S(2)}) collective-permute-start(f32[32,768]{1,0:T(8,128)S(1)} %get-tuple-element.21.token), channel_id=1, source_target_pairs={{0,8},{1,9},{2,10},{3,11},{4,12},{5,13},{6,14},{7,15},{8,0},{9,1},... | collective-permute-start | bytes 294920 | tf_op jit(solution)/shard_map/ppermute | solution.py:338
  50.6 4.9 %shard_map.101.token.near_in = f32[32,1024]{1,0:T(8,128)S(1)} custom-call(s32[1,7]{1,0:T(1,128)S(1)} %copy-done.6, f32[32,1024]{1,0:T(8,128)S(1)} %shard_map.97.token.near_in, bf16[208,1024]{1,0:T(8,128)(2,1)S(1)} %get-tuple-element.16.features, f32[32,768]{1,0:T(8,128)S(1)} %get-tuple-element.21.token, f32[128,1024]{1,0:T(8,128)S(1)} %shard_map.100.refs_0_, ...), custom_call_target="tpu_custom_call" | custom-call | flops 40000000000 | bytes 1048576 | tf_op jit(solution)/shard_map/pallas_call | solution.py:347
  55.5 1.1 %shard_map.102.token.lower = f32[32,1024]{1,0:T(8,128)S(1)} custom-call(s32[1,2,4]{2,1,0:T(2,128)S(1)} %bitcast.6, f32[1,32]{1,0:T(1,128)S(1)} %bitcast.8, f32[128,1024]{1,0:T(8,128)S(1)} %shard_map.91.chip.mine, f32[1,256,1024]{2,1,0:T(8,128)S(1)} %copy-done.2, f32[3,256,1024]{2,1,0:T(8,128)S(1)} %shard_map.95.token.composed, ...), custom_call_target="tpu_custom_call" | custom-call | flops 100000000 | bytes 1048576 | tf_op jit(solution)/shard_map/pallas_call | solution.py:415
  56.6 0.0 collective-permute-done.12.value
  56.6 1.8 %shard_map.104.token.near_in = f32[32,1024]{1,0:T(8,128)S(1)} custom-call(s32[1,7]{1,0:T(1,128)S(1)} %copy-done.6, f32[32,1024]{1,0:T(8,128)S(1)} %shard_map.101.token.near_in, bf16[208,1024]{1,0:T(8,128)(2,1)S(1)} %get-tuple-element.16.features, f32[32,1024]{1,0:T(8,128)S(1)} %shard_map.102.token.lower, f32[128,1024]{1,0:T(8,128)S(1)} %shard_map.103.refs_0_.value), custom_call_target="tpu_custom_call" | custom-call | flops 100000 | bytes 1048576 | tf_op jit(solution)/shard_map/pallas_call | solution.py:347
  58.5 0.1 collective-permute-start.16
  58.6 0.5 collective-permute-start.17
  59.1 1.0 %collective-permute-done.16.refs_0_ = f32[64,1024]{1,0:T(8,128)S(1)} collective-permute-done((f32[64,1024]{1,0:T(8,128)S(1)}, f32[64,1024]{1,0:T(8,128)S(1)}, u32[]{:S(2)}, u32[]{:S(2)}) %collective-permute-start.16) | collective-permute-done | bytes 262176 | tf_op jit(solution)/shard_map/ppermute | solution.py:338
  60.1 1.7 %shard_map.107.near_field = f32[32,1024]{1,0:T(8,128)S(1)} custom-call(s32[1,7]{1,0:T(1,128)S(1)} %copy-done.6, f32[32,1024]{1,0:T(8,128)S(1)} %shard_map.104.token.near_in, bf16[208,1024]{1,0:T(8,128)(2,1)S(1)} %get-tuple-element.16.features, f32[32,1280]{1,0:T(8,128)S(1)} %shard_map.105.token.last, f32[64,1024]{1,0:T(8,128)S(1)} %collective-permute-done.16.refs_0_), custom_call_target="tpu_custom_call" | custom-call | flops 10000000000 | bytes 1048576 | tf_op jit(solution)/shard_map/pallas_call | solution.py:347
  61.9 1.9 %shard_map.108 = f32[32,1024]{1,0:T(8,128)} custom-call(s32[1,2,4]{2,1,0:T(2,128)S(1)} %bitcast.7, f32[3,256,1024]{2,1,0:T(8,128)S(1)} %shard_map.95.token.composed, f32[32,1024]{1,0:T(8,128)S(1)} %shard_map.107.near_field, f32[32,1024]{1,0:T(8,128)S(1)} %shard_map.102.token.lower, f32[32,1280]{1,0:T(8,128)S(1)} %get-tuple-element.23.middle.kept, ...), custom_call_target="tpu_custom_call" | custom-call | flops 1000000000 | bytes 1048576 | tf_op jit(solution)/shard_map/pallas_call | solution.py:439
  (26 shorter events, 0.1 us)
Async XLA Ops:
  0.0 1.6 %collective-permute-start = (f32[32,1024]{1,0:T(8,128)}, f32[32,1024]{1,0:T(8,128)S(1)}, u32[]{:S(2)}, u32[]{:S(2)}) collective-permute-start(f32[32,1024]{1,0:T(8,128)} %points.1), channel_id=1, source_target_pairs={{0,1},{1,0},{2,3},{3,2},{4,5},{5,4},{6,7},{7,6},{8,9},{9,8},{10,11... | collective-permute-start | bytes 393224 | tf_op jit(solution)/shard_map/ppermute | solution.py:338
  0.0 1.7 %collective-permute-start.1 = (f32[32,1024]{1,0:T(8,128)}, f32[32,1024]{1,0:T(8,128)S(1)}, u32[]{:S(2)}, u32[]{:S(2)}) collective-permute-start(f32[32,1024]{1,0:T(8,128)} %charges.1), channel_id=1, source_target_pairs={{0,1},{1,0},{2,3},{3,2},{4,5},{5,4},{6,7},{7,6},{8,9},{9,8},{10,11... | collective-permute-start | bytes 393224 | tf_op jit(solution)/shard_map/ppermute | solution.py:338
  1.7 0.9 %copy-start.3 = (f32[32,1024]{1,0:T(8,128)S(1)}, f32[32,1024]{1,0:T(8,128)}, u32[]{:S(2)}) copy-start(f32[32,1024]{1,0:T(8,128)} %points.1) | copy-start | bytes 393220
  2.7 0.9 %copy-start.4 = (f32[32,1024]{1,0:T(8,128)S(1)}, f32[32,1024]{1,0:T(8,128)}, u32[]{:S(2)}) copy-start(f32[32,1024]{1,0:T(8,128)} %charges.1) | copy-start | bytes 393220
  3.6 16.9 %copy-start.5 = (s32[1,3,256]{2,0,1:T(1,128)S(1)}, s32[1,3,256]{2,0,1:T(1,128)}, u32[]{:S(2)}) copy-start(s32[1,3,256]{2,0,1:T(1,128)} %param.12) | copy-start | bytes 9220
  3.6 17.1 %copy-start.6 = (s32[1,7]{1,0:T(1,128)S(1)}, s32[1,7]{1,0:T(1,128)}, u32[]{:S(2)}) copy-start(s32[1,7]{1,0:T(1,128)} %near.9) | copy-start | bytes 88
  3.6 16.9 %copy-start = (f32[1,3,256,512]{3,2,1,0:T(8,128)S(1)}, f32[1,3,256,512]{3,2,1,0:T(8,128)}, u32[]{:S(2)}) copy-start(f32[1,3,256,512]{3,2,1,0:T(8,128)} %matrix.7) | copy-start | bytes 4718596
  3.6 21.3 %collective-permute-start.3 = (f32[128,1024]{1,0:T(8,128)S(1)}, f32[128,1024]{1,0:T(8,128)S(1)}, u32[]{:S(2)}, u32[]{:S(2)}) collective-permute-start(f32[128,1024]{1,0:T(8,128)S(1)} %shard_map.91.chip.mine), channel_id=1, source_target_pairs={{0,4},{2,6},{4,8},{5,1},{6,10},{7,3},{8,12},{9,5},{10,14},{11,7},{... | collective-permute-start | bytes 1572872 | tf_op jit(solution)/shard_map/ppermute | solution.py:343
  8.9 23.8 %collective-permute-start.8 = (f32[128,1024]{1,0:T(8,128)S(1)}, f32[128,1024]{1,0:T(8,128)S(1)}, u32[]{:S(2)}, u32[]{:S(2)}) collective-permute-start(f32[128,1024]{1,0:T(8,128)S(1)} %shard_map.91.chip.mine), channel_id=1, source_target_pairs={{0,2},{2,4},{3,1},{4,6},{5,3},{6,8},{7,5},{8,10},{9,7},{10,12},{11... | collective-permute-start | bytes 1572872 | tf_op jit(solution)/shard_map/ppermute | solution.py:343
  12.8 1.2 %copy-start.1 = (f32[1,256,1024]{2,1,0:T(8,128)S(1)}, f32[1,256,1024]{2,1,0:T(8,128)}, u32[]{:S(2)}) copy-start(f32[1,256,1024]{2,1,0:T(8,128)} %leaf_matrix.3) | copy-start | bytes 3145732
  14.0 0.7 %copy-start.9 = (s32[1,256]{1,0:T(1,128)S(1)}, s32[1,256]{1,0:T(1,128)}, u32[]{:S(2)}) copy-start(s32[1,256]{1,0:T(1,128)} %chosen.1) | copy-start | bytes 3076
  15.2 7.0 %copy-start.2 = (f32[1,256,1024]{2,1,0:T(8,128)S(1)}, f32[1,256,1024]{2,1,0:T(8,128)}, u32[]{:S(2)}) copy-start(f32[1,256,1024]{2,1,0:T(8,128)} %leaf_matrix.3) | copy-start | bytes 3145732
  15.2 5.2 %collective-permute-start.2 = (f32[64,256]{1,0:T(8,128)S(1)}, f32[64,256]{1,0:T(8,128)S(1)}, u32[]{:S(2)}, u32[]{:S(2)}) collective-permute-start(f32[64,256]{1,0:T(8,128)S(1)} %shard_map.92.own.token.leaf_own), channel_id=1, source_target_pairs={{0,1},{1,0},{2,3},{3,2},{4,5},{5,4},{6,7},{7,6},{8,9},{9,8},{10,11... | collective-permute-start | bytes 196616 | tf_op jit(solution)/shard_map/ppermute | solution.py:338
  25.0 3.9 %collective-permute-start.4 = (f32[64,1024]{1,0:T(8,128)S(1)}, f32[64,1024]{1,0:T(8,128)S(1)}, u32[]{:S(2)}, u32[]{:S(2)}) collective-permute-start(f32[64,1024]{1,0:T(8,128)S(1)} %get-tuple-element.18), channel_id=1, source_target_pairs={{0,1},{1,0},{2,3},{3,2},{4,5},{5,4},{6,7},{7,6},{8,9},{9,8},{10,11... | collective-permute-start | bytes 786440 | tf_op jit(solution)/shard_map/ppermute | solution.py:338
  26.3 2.6 %collective-permute-start.5 = (f32[64,1024]{1,0:T(8,128)S(1)}, f32[64,1024]{1,0:T(8,128)S(1)}, u32[]{:S(2)}, u32[]{:S(2)}) collective-permute-start(f32[64,1024]{1,0:T(8,128)S(1)} %get-tuple-element.19), channel_id=1, source_target_pairs={{0,1},{1,0},{2,3},{3,2},{4,5},{5,4},{6,7},{7,6},{8,9},{9,8},{10,11... | collective-permute-start | bytes 786440 | tf_op jit(solution)/shard_map/ppermute | solution.py:338
  26.4 6.2 %collective-permute-start.6 = (f32[32,768]{1,0:T(8,128)S(1)}, f32[32,768]{1,0:T(8,128)S(1)}, u32[]{:S(2)}, u32[]{:S(2)}) collective-permute-start(f32[32,768]{1,0:T(8,128)S(1)} %shard_map.93.token.own), channel_id=1, source_target_pairs={{0,2},{1,3},{2,0},{3,1},{4,6},{5,7},{6,4},{7,5},{8,10},{9,11},{10,... | collective-permute-start | bytes 294920 | tf_op jit(solution)/shard_map/ppermute | solution.py:338
  32.8 13.9 %collective-permute-start.9 = (f32[128,1024]{1,0:T(8,128)S(1)}, f32[128,1024]{1,0:T(8,128)S(1)}, u32[]{:S(2)}, u32[]{:S(2)}) collective-permute-start(f32[128,1024]{1,0:T(8,128)S(1)} %shard_map.100.refs_0_), channel_id=1, source_target_pairs={{0,1},{1,0},{2,3},{3,2},{4,5},{5,4},{6,7},{7,6},{8,9},{9,8},{10,11... | collective-permute-start | bytes 1572872 | tf_op jit(solution)/shard_map/ppermute | solution.py:338
  34.0 12.7 %collective-permute-start.10 = (f32[32,1024]{1,0:T(8,128)S(1)}, f32[32,1024]{1,0:T(8,128)S(1)}, u32[]{:S(2)}, u32[]{:S(2)}) collective-permute-start(f32[32,1024]{1,0:T(8,128)S(1)} %get-tuple-element.22.low), channel_id=1, source_target_pairs={{0,1},{1,0},{2,3},{3,2},{4,5},{5,4},{6,7},{7,6},{8,9},{9,8},{10,11... | collective-permute-start | bytes 393224 | tf_op jit(solution)/shard_map/ppermute | solution.py:338
  34.1 8.6 %collective-permute-start.7 = (f32[32,768]{1,0:T(8,128)S(1)}, f32[32,768]{1,0:T(8,128)S(1)}, u32[]{:S(2)}, u32[]{:S(2)}) collective-permute-start(f32[32,768]{1,0:T(8,128)S(1)} %get-tuple-element.20.own.token), channel_id=1, source_target_pairs={{0,4},{1,5},{2,6},{3,7},{4,0},{5,1},{6,2},{7,3},{8,12},{9,13},{10,... | collective-permute-start | bytes 294920 | tf_op jit(solution)/shard_map/ppermute | solution.py:338
  34.2 22.4 %collective-permute-start.12 = (f32[128,1024]{1,0:T(8,128)S(1)}, f32[128,1024]{1,0:T(8,128)S(1)}, u32[]{:S(2)}, u32[]{:S(2)}) collective-permute-start(f32[128,1024]{1,0:T(8,128)S(1)} %get-tuple-element.17.refs_0_), channel_id=1, source_target_pairs={{0,2},{2,4},{3,1},{4,6},{5,3},{6,8},{7,5},{8,10},{9,7},{10,12},{11... | collective-permute-start | bytes 1572872 | tf_op jit(solution)/shard_map/ppermute | solution.py:343
  43.0 15.5 %collective-permute-start.14 = (f32[32,256]{1,0:T(8,128)S(1)}, f32[32,256]{1,0:T(8,128)S(1)}, u32[]{:S(2)}, u32[]{:S(2)}) collective-permute-start(f32[32,256]{1,0:T(8,128)S(1)} %get-tuple-element.24), channel_id=1, source_target_pairs={{0,16},{1,17},{2,18},{3,19},{4,20},{5,21},{6,22},{7,23},{8,24},{9,... | collective-permute-start | bytes 98312 | tf_op jit(solution)/shard_map/ppermute | solution.py:338
  43.1 15.4 %collective-permute-start.15 = (f32[32,256]{1,0:T(8,128)S(1)}, f32[32,256]{1,0:T(8,128)S(1)}, u32[]{:S(2)}, u32[]{:S(2)}) collective-permute-start(f32[32,256]{1,0:T(8,128)S(1)} %get-tuple-element.24), channel_id=1, source_target_pairs={{0,24},{1,25},{2,26},{3,27},{4,28},{5,29},{6,30},{7,31},{8,16},{9,... | collective-permute-start | bytes 98312 | tf_op jit(solution)/shard_map/ppermute | solution.py:338
  46.7 8.8 %collective-permute-start.11 = (f32[32,1280]{1,0:T(8,128)S(1)}, f32[32,1280]{1,0:T(8,128)S(1)}, u32[]{:S(2)}, u32[]{:S(2)}) collective-permute-start(f32[32,1280]{1,0:T(8,128)S(1)} %get-tuple-element.23.middle.kept), channel_id=1, source_target_pairs={{0,1},{1,0},{2,3},{3,2},{4,5},{5,4},{6,7},{7,6},{8,9},{9,8},{10,11... | collective-permute-start | bytes 491528 | tf_op jit(solution)/shard_map/ppermute | solution.py:338
  46.7 8.8 %copy-start.7 = (s32[1,4,2]{1,2,0:T(2,128)S(1)}, s32[1,4,2]{1,2,0:T(2,128)}, u32[]{:S(2)}) copy-start(s32[1,4,2]{1,2,0:T(2,128)} %param.16) | copy-start | bytes 100
  46.7 8.8 %copy-start.8 = (f32[32]{0:T(128)S(1)}, f32[32]{0:T(128)}, u32[]{:S(2)}) copy-start(f32[32]{0:T(128)} %param.17) | copy-start | bytes 388
  46.7 11.7 %collective-permute-start.13 = (f32[32,768]{1,0:T(8,128)S(1)}, f32[32,768]{1,0:T(8,128)S(1)}, u32[]{:S(2)}, u32[]{:S(2)}) collective-permute-start(f32[32,768]{1,0:T(8,128)S(1)} %get-tuple-element.21.token), channel_id=1, source_target_pairs={{0,8},{1,9},{2,10},{3,11},{4,12},{5,13},{6,14},{7,15},{8,0},{9,1},... | collective-permute-start | bytes 294920 | tf_op jit(solution)/shard_map/ppermute | solution.py:338
  58.5 1.6 %collective-permute-start.16 = (f32[64,1024]{1,0:T(8,128)S(1)}, f32[64,1024]{1,0:T(8,128)S(1)}, u32[]{:S(2)}, u32[]{:S(2)}) collective-permute-start(f32[64,1024]{1,0:T(8,128)S(1)} %shard_map.106), channel_id=1, source_target_pairs={{0,1},{1,0},{2,3},{3,2},{4,5},{5,4},{6,7},{7,6},{8,9},{9,8},{10,11... | collective-permute-start | bytes 786440 | tf_op jit(solution)/shard_map/ppermute | solution.py:338
  58.6 3.3 %collective-permute-start.17 = (f32[32,1280]{1,0:T(8,128)S(1)}, f32[32,1280]{1,0:T(8,128)S(1)}, u32[]{:S(2)}, u32[]{:S(2)}) collective-permute-start(f32[32,1280]{1,0:T(8,128)S(1)} %shard_map.105.token.last), channel_id=1, source_target_pairs={{0,1},{1,0},{2,3},{3,2},{4,5},{5,4},{6,7},{7,6},{8,9},{9,8},{10,11... | collective-permute-start | bytes 491528 | tf_op jit(solution)/shard_map/ppermute | solution.py:338

commit v3 on v2

--- a/solution.py
+++ b/solution.py
@@ -384,7 +384,7 @@
         near_first,
         [shape(32, size), shape(208, size, bf16)],
         [VMEM] * 2 + [ANY],
-        10**5,
+        2 * 10**9,
         [pltpu.VMEM((96, size), f32)],
     )(near_leaves, chip, sent1)
     composed = call(

time: 64 us -> 63.9 us (level)
  starting transfers between devices: 31.8 us -> 31.1 us
    pallas_call x4, Pallas kernels: 10.3 us -> 8.72 us  [near_step(): call(functools.partial(near_blocks, entries, count), shape(32, size), [VM...]
    pallas_call x1, Pallas kernels: 1.54 us -> 3.09 us  [body(): call(near_first, [shape(32, size), shape(208, size, bf16)], [VMEM] * 2 +...]
    ppermute x3, starting transfers between devices: 13.5 us -> 12.6 us  [along(): return lax.ppermute(value, 'leaf', pairs)]
where the time goes in v3:
time: 63.9 us; the launch traced here: 63.2 us
  starting transfers between devices  31.1 us (49%)
  Pallas kernels  18.6 us (29%)
  waiting for transfers between devices  9.41 us (15%)
  local copies, waits for them, and re-layouts  3.76 us (6%)
    ppermute x15, starting transfers between devices, partner(): lax.ppermute(value, 'leaf', [(leaf, leaf ^ bit) for leaf in range(devices)])  18.5 us
    ppermute x3, starting transfers between devices, along(): return lax.ppermute(value, 'leaf', pairs)  12.6 us
    ppermute x15, waiting for transfers between devices, partner(): lax.ppermute(value, 'leaf', [(leaf, leaf ^ bit) for leaf in range(devices)])  9.37 us
    pallas_call x4, Pallas kernels, near_step(): call(functools.partial(near_blocks, entries, count), shape(32, size), [VM...  8.72 us
    unnamed x20, local copies, waits for them, and re-layouts  3.76 us
    pallas_call x1, Pallas kernels, body(): call(near_first, [shape(32, size), shape(208, size, bf16)], [VMEM] * 2 +...  3.09 us
    pallas_call x1, Pallas kernels, body(): call(compose, jax.ShapeDtypeStruct((3, RANK, size), f32), [VMEM, VMEM, AN...  2.64 us
    pallas_call x1, Pallas kernels, body(): call(finish, shape(32, size), [VMEM] * 8, 10 ** 9)  1.88 us
  transfers between devices with their start and end apart: 18, of which 6 were waited for; matrix products, arithmetic and copies ran while one was open for 0% of the time, Pallas kernels for 26%

profile of v3, /device:TPU:24, one launch (start us, length us, event | category | flops | bytes accessed | tf_op | source)
XLA Modules:
  0.0 63.2 jit_solution(12864193836645896055)
XLA Ops:
  0.0 0.0 collective-permute-start
  0.0 0.5 collective-permute-start.1
  0.5 1.0 %collective-permute-done.other_points = f32[32,1024]{1,0:T(8,128)S(1)} collective-permute-done((f32[32,1024]{1,0:T(8,128)}, f32[32,1024]{1,0:T(8,128)S(1)}, u32[]{:S(2)}, u32[]{:S(2)}) %collective-permute-start) | collective-permute-done | bytes 131104 | tf_op jit(solution)/shard_map/ppermute | solution.py:338
  1.6 0.2 collective-permute-done.1.other_charges
  1.7 0.9 %copy-done.3 = f32[32,1024]{1,0:T(8,128)S(1)} copy-done((f32[32,1024]{1,0:T(8,128)S(1)}, f32[32,1024]{1,0:T(8,128)}, u32[]{:S(2)}) %copy-start.3) | copy-done | bytes 131096
  2.7 0.9 %copy-done.4 = f32[32,1024]{1,0:T(8,128)S(1)} copy-done((f32[32,1024]{1,0:T(8,128)S(1)}, f32[32,1024]{1,0:T(8,128)}, u32[]{:S(2)}) %copy-start.4) | copy-done | bytes 131096
  3.6 0.0 copy-start
  3.6 5.3 %collective-permute-start.3 = (f32[128,1024]{1,0:T(8,128)S(1)}, f32[128,1024]{1,0:T(8,128)S(1)}, u32[]{:S(2)}, u32[]{:S(2)}) collective-permute-start(f32[128,1024]{1,0:T(8,128)S(1)} %shard_map.91.chip.mine), channel_id=1, source_target_pairs={{0,4},{2,6},{4,8},{5,1},{6,10},{7,3},{8,12},{9,5},{10,14},{11,7},{... | collective-permute-start | bytes 1572872 | tf_op jit(solution)/shard_map/ppermute | solution.py:343
  8.9 0.0 copy-start.1
  8.9 1.2 %copy-done.1 = f32[1,256,1024]{2,1,0:T(8,128)S(1)} copy-done((f32[1,256,1024]{2,1,0:T(8,128)S(1)}, f32[1,256,1024]{2,1,0:T(8,128)}, u32[]{:S(2)}) %copy-start.1) | copy-done | bytes 1048600
  10.2 0.7 %copy-done.9 = s32[1,256]{1,0:T(1,128)S(1)} copy-done((s32[1,256]{1,0:T(1,128)S(1)}, s32[1,256]{1,0:T(1,128)}, u32[]{:S(2)}) %copy-start.9) | copy-done | bytes 1048
  10.8 0.5 shard_map.92.own.token.leaf_own
  11.4 5.5 %collective-permute-start.2 = (f32[64,256]{1,0:T(8,128)S(1)}, f32[64,256]{1,0:T(8,128)S(1)}, u32[]{:S(2)}, u32[]{:S(2)}) collective-permute-start(f32[64,256]{1,0:T(8,128)S(1)} %shard_map.92.own.token.leaf_own), channel_id=1, source_target_pairs={{0,1},{1,0},{2,3},{3,2},{4,5},{5,4},{6,7},{7,6},{8,9},{9,8},{10,11... | collective-permute-start | bytes 196616 | tf_op jit(solution)/shard_map/ppermute | solution.py:338
  16.9 2.9 %collective-permute-start.8 = (f32[128,1024]{1,0:T(8,128)S(1)}, f32[128,1024]{1,0:T(8,128)S(1)}, u32[]{:S(2)}, u32[]{:S(2)}) collective-permute-start(f32[128,1024]{1,0:T(8,128)S(1)} %shard_map.91.chip.mine), channel_id=1, source_target_pairs={{0,2},{2,4},{3,1},{4,6},{5,3},{6,8},{7,5},{8,10},{9,7},{10,12},{11... | collective-permute-start | bytes 1572872 | tf_op jit(solution)/shard_map/ppermute | solution.py:343
  19.8 0.2 shard_map.93.token.own
  20.0 0.0 copy-done.7
  20.1 0.0 copy-start.2
  20.1 3.1 %shard_map.94 = (f32[32,1024]{1,0:T(8,128)S(1)}, bf16[208,1024]{1,0:T(8,128)(2,1)S(1)}) custom-call(s32[1,7]{1,0:T(1,128)S(1)} %copy-done.7, f32[128,1024]{1,0:T(8,128)S(1)} %shard_map.91.chip.mine, f32[32,768]{1,0:T(8,128)S(1)} %shard_map.93.token.own), custom_call_target="tpu_custom_call" | custom-call | flops 2000000000 | bytes 1048576 | tf_op jit(solution)/shard_map/pallas_call | solution.py:383
  23.2 2.6 %shard_map.95.token.composed = f32[3,256,1024]{2,1,0:T(8,128)S(1)} custom-call(f32[1,3,256,512]{3,2,1,0:T(8,128)S(1)} %copy-done, f32[1,256,1024]{2,1,0:T(8,128)S(1)} %copy-done.2, f32[32,1024]{1,0:T(8,128)S(1)} %get-tuple-element.15.token.near_in), custom_call_target="tpu_custom_call" | custom-call | flops 100000 | bytes 1048576 | tf_op jit(solution)/shard_map/pallas_call | solution.py:390
  25.8 0.1 shard_map.96
  25.9 0.3 collective-permute-start.4
  26.3 0.3 collective-permute-start.5
  26.5 2.3 %collective-permute-start.6 = (f32[32,768]{1,0:T(8,128)S(1)}, f32[32,768]{1,0:T(8,128)S(1)}, u32[]{:S(2)}, u32[]{:S(2)}) collective-permute-start(f32[32,768]{1,0:T(8,128)S(1)} %shard_map.93.token.own), channel_id=1, source_target_pairs={{0,2},{1,3},{2,0},{3,1},{4,6},{5,7},{6,4},{7,5},{8,10},{9,11},{10,... | collective-permute-start | bytes 294920 | tf_op jit(solution)/shard_map/ppermute | solution.py:338
  28.8 0.3 shard_map.97.token.near_in
  29.1 3.4 %collective-permute-done.6.sibling = f32[32,768]{1,0:T(8,128)S(1)} collective-permute-done((f32[32,768]{1,0:T(8,128)S(1)}, f32[32,768]{1,0:T(8,128)S(1)}, u32[]{:S(2)}, u32[]{:S(2)}) %collective-permute-start.6) | collective-permute-done | bytes 98336 | tf_op jit(solution)/shard_map/ppermute | solution.py:338
  32.5 0.2 shard_map.98
  32.7 0.0 collective-permute-done.8.value
  32.8 0.4 collective-permute-start.9
  33.2 0.2 collective-permute-start.10
  33.4 0.8 %collective-permute-start.7 = (f32[32,768]{1,0:T(8,128)S(1)}, f32[32,768]{1,0:T(8,128)S(1)}, u32[]{:S(2)}, u32[]{:S(2)}) collective-permute-start(f32[32,768]{1,0:T(8,128)S(1)} %get-tuple-element.20.own.token), channel_id=1, source_target_pairs={{0,4},{1,5},{2,6},{3,7},{4,0},{5,1},{6,2},{7,3},{8,12},{9,13},{10,... | collective-permute-start | bytes 294920 | tf_op jit(solution)/shard_map/ppermute | solution.py:338
  34.2 4.4 %collective-permute-start.12 = (f32[128,1024]{1,0:T(8,128)S(1)}, f32[128,1024]{1,0:T(8,128)S(1)}, u32[]{:S(2)}, u32[]{:S(2)}) collective-permute-start(f32[128,1024]{1,0:T(8,128)S(1)} %get-tuple-element.17.refs_0_), channel_id=1, source_target_pairs={{0,2},{2,4},{3,1},{4,6},{5,3},{6,8},{7,5},{8,10},{9,7},{10,12},{11... | collective-permute-start | bytes 1572872 | tf_op jit(solution)/shard_map/ppermute | solution.py:343
  38.6 3.4 %collective-permute-done.7.sibling = f32[32,768]{1,0:T(8,128)S(1)} collective-permute-done((f32[32,768]{1,0:T(8,128)S(1)}, f32[32,768]{1,0:T(8,128)S(1)}, u32[]{:S(2)}, u32[]{:S(2)}) %collective-permute-start.7) | collective-permute-done | bytes 98336 | tf_op jit(solution)/shard_map/ppermute | solution.py:338
  41.9 0.2 shard_map.99
  42.1 0.1 collective-permute-start.14
  42.2 5.0 %collective-permute-start.15 = (f32[32,256]{1,0:T(8,128)S(1)}, f32[32,256]{1,0:T(8,128)S(1)}, u32[]{:S(2)}, u32[]{:S(2)}) collective-permute-start(f32[32,256]{1,0:T(8,128)S(1)} %get-tuple-element.24), channel_id=1, source_target_pairs={{0,24},{1,25},{2,26},{3,27},{4,28},{5,29},{6,30},{7,31},{8,16},{9,... | collective-permute-start | bytes 98312 | tf_op jit(solution)/shard_map/ppermute | solution.py:338
  47.3 0.0 copy-start.6
  47.3 0.0 copy-start.8
  47.3 2.5 %collective-permute-start.13 = (f32[32,768]{1,0:T(8,128)S(1)}, f32[32,768]{1,0:T(8,128)S(1)}, u32[]{:S(2)}, u32[]{:S(2)}) collective-permute-start(f32[32,768]{1,0:T(8,128)S(1)} %get-tuple-element.21.token), channel_id=1, source_target_pairs={{0,8},{1,9},{2,10},{3,11},{4,12},{5,13},{6,14},{7,15},{8,0},{9,1},... | collective-permute-start | bytes 294920 | tf_op jit(solution)/shard_map/ppermute | solution.py:338
  49.8 4.9 %shard_map.101.token.near_in = f32[32,1024]{1,0:T(8,128)S(1)} custom-call(s32[1,7]{1,0:T(1,128)S(1)} %copy-done.7, f32[32,1024]{1,0:T(8,128)S(1)} %shard_map.97.token.near_in, bf16[208,1024]{1,0:T(8,128)(2,1)S(1)} %get-tuple-element.16.features, f32[32,768]{1,0:T(8,128)S(1)} %get-tuple-element.21.token, f32[128,1024]{1,0:T(8,128)S(1)} %shard_map.100.refs_0_, ...), custom_call_target="tpu_custom_call" | custom-call | flops 40000000000 | bytes 1048576 | tf_op jit(solution)/shard_map/pallas_call | solution.py:347
  54.7 1.1 %shard_map.102.token.lower = f32[32,1024]{1,0:T(8,128)S(1)} custom-call(s32[1,2,4]{2,1,0:T(2,128)S(1)} %bitcast.6, f32[1,32]{1,0:T(1,128)S(1)} %bitcast.8, f32[128,1024]{1,0:T(8,128)S(1)} %shard_map.91.chip.mine, f32[1,256,1024]{2,1,0:T(8,128)S(1)} %copy-done.2, f32[3,256,1024]{2,1,0:T(8,128)S(1)} %shard_map.95.token.composed, ...), custom_call_target="tpu_custom_call" | custom-call | flops 100000000 | bytes 1048576 | tf_op jit(solution)/shard_map/pallas_call | solution.py:415
  55.8 0.0 collective-permute-done.12.value
  55.8 1.8 %shard_map.104.token.near_in = f32[32,1024]{1,0:T(8,128)S(1)} custom-call(s32[1,7]{1,0:T(1,128)S(1)} %copy-done.7, f32[32,1024]{1,0:T(8,128)S(1)} %shard_map.101.token.near_in, bf16[208,1024]{1,0:T(8,128)(2,1)S(1)} %get-tuple-element.16.features, f32[32,1024]{1,0:T(8,128)S(1)} %shard_map.102.token.lower, f32[128,1024]{1,0:T(8,128)S(1)} %shard_map.103.refs_0_.value), custom_call_target="tpu_custom_call" | custom-call | flops 100000 | bytes 1048576 | tf_op jit(solution)/shard_map/pallas_call | solution.py:347
  57.6 0.3 collective-permute-done.13.far_one
  58.0 0.1 collective-permute-start.16
  58.1 0.5 collective-permute-start.17
  58.6 1.0 %collective-permute-done.16.refs_0_ = f32[64,1024]{1,0:T(8,128)S(1)} collective-permute-done((f32[64,1024]{1,0:T(8,128)S(1)}, f32[64,1024]{1,0:T(8,128)S(1)}, u32[]{:S(2)}, u32[]{:S(2)}) %collective-permute-start.16) | collective-permute-done | bytes 262176 | tf_op jit(solution)/shard_map/ppermute | solution.py:338
  59.6 1.7 %shard_map.107.near_field = f32[32,1024]{1,0:T(8,128)S(1)} custom-call(s32[1,7]{1,0:T(1,128)S(1)} %copy-done.7, f32[32,1024]{1,0:T(8,128)S(1)} %shard_map.104.token.near_in, bf16[208,1024]{1,0:T(8,128)(2,1)S(1)} %get-tuple-element.16.features, f32[32,1280]{1,0:T(8,128)S(1)} %shard_map.105.token.last, f32[64,1024]{1,0:T(8,128)S(1)} %collective-permute-done.16.refs_0_), custom_call_target="tpu_custom_call" | custom-call | flops 10000000000 | bytes 1048576 | tf_op jit(solution)/shard_map/pallas_call | solution.py:347
  61.4 1.9 %shard_map.108 = f32[32,1024]{1,0:T(8,128)} custom-call(s32[1,2,4]{2,1,0:T(2,128)S(1)} %bitcast.7, f32[3,256,1024]{2,1,0:T(8,128)S(1)} %shard_map.95.token.composed, f32[32,1024]{1,0:T(8,128)S(1)} %shard_map.107.near_field, f32[32,1024]{1,0:T(8,128)S(1)} %shard_map.102.token.lower, f32[32,1280]{1,0:T(8,128)S(1)} %get-tuple-element.23.middle.kept, ...), custom_call_target="tpu_custom_call" | custom-call | flops 1000000000 | bytes 1048576 | tf_op jit(solution)/shard_map/pallas_call | solution.py:439
  (26 shorter events, 0.1 us)
Async XLA Ops:
  0.0 1.6 %collective-permute-start = (f32[32,1024]{1,0:T(8,128)}, f32[32,1024]{1,0:T(8,128)S(1)}, u32[]{:S(2)}, u32[]{:S(2)}) collective-permute-start(f32[32,1024]{1,0:T(8,128)} %points.1), channel_id=1, source_target_pairs={{0,1},{1,0},{2,3},{3,2},{4,5},{5,4},{6,7},{7,6},{8,9},{9,8},{10,11... | collective-permute-start | bytes 393224 | tf_op jit(solution)/shard_map/ppermute | solution.py:338
  0.0 1.7 %collective-permute-start.1 = (f32[32,1024]{1,0:T(8,128)}, f32[32,1024]{1,0:T(8,128)S(1)}, u32[]{:S(2)}, u32[]{:S(2)}) collective-permute-start(f32[32,1024]{1,0:T(8,128)} %charges.1), channel_id=1, source_target_pairs={{0,1},{1,0},{2,3},{3,2},{4,5},{5,4},{6,7},{7,6},{8,9},{9,8},{10,11... | collective-permute-start | bytes 393224 | tf_op jit(solution)/shard_map/ppermute | solution.py:338
  1.7 0.9 %copy-start.3 = (f32[32,1024]{1,0:T(8,128)S(1)}, f32[32,1024]{1,0:T(8,128)}, u32[]{:S(2)}) copy-start(f32[32,1024]{1,0:T(8,128)} %points.1) | copy-start | bytes 393220
  2.7 0.9 %copy-start.4 = (f32[32,1024]{1,0:T(8,128)S(1)}, f32[32,1024]{1,0:T(8,128)}, u32[]{:S(2)}) copy-start(f32[32,1024]{1,0:T(8,128)} %charges.1) | copy-start | bytes 393220
  3.6 16.2 %copy-start = (f32[1,3,256,512]{3,2,1,0:T(8,128)S(1)}, f32[1,3,256,512]{3,2,1,0:T(8,128)}, u32[]{:S(2)}) copy-start(f32[1,3,256,512]{3,2,1,0:T(8,128)} %matrix.7) | copy-start | bytes 4718596
  3.6 22.2 %collective-permute-start.3 = (f32[128,1024]{1,0:T(8,128)S(1)}, f32[128,1024]{1,0:T(8,128)S(1)}, u32[]{:S(2)}, u32[]{:S(2)}) collective-permute-start(f32[128,1024]{1,0:T(8,128)S(1)} %shard_map.91.chip.mine), channel_id=1, source_target_pairs={{0,4},{2,6},{4,8},{5,1},{6,10},{7,3},{8,12},{9,5},{10,14},{11,7},{... | collective-permute-start | bytes 1572872 | tf_op jit(solution)/shard_map/ppermute | solution.py:343
  8.9 1.2 %copy-start.1 = (f32[1,256,1024]{2,1,0:T(8,128)S(1)}, f32[1,256,1024]{2,1,0:T(8,128)}, u32[]{:S(2)}) copy-start(f32[1,256,1024]{2,1,0:T(8,128)} %leaf_matrix.3) | copy-start | bytes 3145732
  10.2 0.7 %copy-start.9 = (s32[1,256]{1,0:T(1,128)S(1)}, s32[1,256]{1,0:T(1,128)}, u32[]{:S(2)}) copy-start(s32[1,256]{1,0:T(1,128)} %chosen.1) | copy-start | bytes 3076
  10.8 9.0 %copy-start.5 = (s32[1,3,256]{2,0,1:T(1,128)S(1)}, s32[1,3,256]{2,0,1:T(1,128)}, u32[]{:S(2)}) copy-start(s32[1,3,256]{2,0,1:T(1,128)} %param.12) | copy-start | bytes 9220
  10.8 9.2 %copy-start.7 = (s32[1,7]{1,0:T(1,128)S(1)}, s32[1,7]{1,0:T(1,128)}, u32[]{:S(2)}) copy-start(s32[1,7]{1,0:T(1,128)} %near.9) | copy-start | bytes 88
  11.4 8.5 %collective-permute-start.2 = (f32[64,256]{1,0:T(8,128)S(1)}, f32[64,256]{1,0:T(8,128)S(1)}, u32[]{:S(2)}, u32[]{:S(2)}) collective-permute-start(f32[64,256]{1,0:T(8,128)S(1)} %shard_map.92.own.token.leaf_own), channel_id=1, source_target_pairs={{0,1},{1,0},{2,3},{3,2},{4,5},{5,4},{6,7},{7,6},{8,9},{9,8},{10,11... | collective-permute-start | bytes 196616 | tf_op jit(solution)/shard_map/ppermute | solution.py:338
  16.9 15.9 %collective-permute-start.8 = (f32[128,1024]{1,0:T(8,128)S(1)}, f32[128,1024]{1,0:T(8,128)S(1)}, u32[]{:S(2)}, u32[]{:S(2)}) collective-permute-start(f32[128,1024]{1,0:T(8,128)S(1)} %shard_map.91.chip.mine), channel_id=1, source_target_pairs={{0,2},{2,4},{3,1},{4,6},{5,3},{6,8},{7,5},{8,10},{9,7},{10,12},{11... | collective-permute-start | bytes 1572872 | tf_op jit(solution)/shard_map/ppermute | solution.py:343
  20.1 3.1 %copy-start.2 = (f32[1,256,1024]{2,1,0:T(8,128)S(1)}, f32[1,256,1024]{2,1,0:T(8,128)}, u32[]{:S(2)}) copy-start(f32[1,256,1024]{2,1,0:T(8,128)} %leaf_matrix.3) | copy-start | bytes 3145732
  25.9 2.9 %collective-permute-start.4 = (f32[64,1024]{1,0:T(8,128)S(1)}, f32[64,1024]{1,0:T(8,128)S(1)}, u32[]{:S(2)}, u32[]{:S(2)}) collective-permute-start(f32[64,1024]{1,0:T(8,128)S(1)} %get-tuple-element.18), channel_id=1, source_target_pairs={{0,1},{1,0},{2,3},{3,2},{4,5},{5,4},{6,7},{7,6},{8,9},{9,8},{10,11... | collective-permute-start | bytes 786440 | tf_op jit(solution)/shard_map/ppermute | solution.py:338
  26.3 2.6 %collective-permute-start.5 = (f32[64,1024]{1,0:T(8,128)S(1)}, f32[64,1024]{1,0:T(8,128)S(1)}, u32[]{:S(2)}, u32[]{:S(2)}) collective-permute-start(f32[64,1024]{1,0:T(8,128)S(1)} %get-tuple-element.19), channel_id=1, source_target_pairs={{0,1},{1,0},{2,3},{3,2},{4,5},{5,4},{6,7},{7,6},{8,9},{9,8},{10,11... | collective-permute-start | bytes 786440 | tf_op jit(solution)/shard_map/ppermute | solution.py:338
  26.5 6.0 %collective-permute-start.6 = (f32[32,768]{1,0:T(8,128)S(1)}, f32[32,768]{1,0:T(8,128)S(1)}, u32[]{:S(2)}, u32[]{:S(2)}) collective-permute-start(f32[32,768]{1,0:T(8,128)S(1)} %shard_map.93.token.own), channel_id=1, source_target_pairs={{0,2},{1,3},{2,0},{3,1},{4,6},{5,7},{6,4},{7,5},{8,10},{9,11},{10,... | collective-permute-start | bytes 294920 | tf_op jit(solution)/shard_map/ppermute | solution.py:338
  32.8 14.5 %collective-permute-start.9 = (f32[128,1024]{1,0:T(8,128)S(1)}, f32[128,1024]{1,0:T(8,128)S(1)}, u32[]{:S(2)}, u32[]{:S(2)}) collective-permute-start(f32[128,1024]{1,0:T(8,128)S(1)} %shard_map.100.refs_0_), channel_id=1, source_target_pairs={{0,1},{1,0},{2,3},{3,2},{4,5},{5,4},{6,7},{7,6},{8,9},{9,8},{10,11... | collective-permute-start | bytes 1572872 | tf_op jit(solution)/shard_map/ppermute | solution.py:338
  33.2 14.1 %collective-permute-start.10 = (f32[32,1024]{1,0:T(8,128)S(1)}, f32[32,1024]{1,0:T(8,128)S(1)}, u32[]{:S(2)}, u32[]{:S(2)}) collective-permute-start(f32[32,1024]{1,0:T(8,128)S(1)} %get-tuple-element.22.low), channel_id=1, source_target_pairs={{0,1},{1,0},{2,3},{3,2},{4,5},{5,4},{6,7},{7,6},{8,9},{9,8},{10,11... | collective-permute-start | bytes 393224 | tf_op jit(solution)/shard_map/ppermute | solution.py:338
  33.4 8.6 %collective-permute-start.7 = (f32[32,768]{1,0:T(8,128)S(1)}, f32[32,768]{1,0:T(8,128)S(1)}, u32[]{:S(2)}, u32[]{:S(2)}) collective-permute-start(f32[32,768]{1,0:T(8,128)S(1)} %get-tuple-element.20.own.token), channel_id=1, source_target_pairs={{0,4},{1,5},{2,6},{3,7},{4,0},{5,1},{6,2},{7,3},{8,12},{9,13},{10,... | collective-permute-start | bytes 294920 | tf_op jit(solution)/shard_map/ppermute | solution.py:338
  34.2 21.6 %collective-permute-start.12 = (f32[128,1024]{1,0:T(8,128)S(1)}, f32[128,1024]{1,0:T(8,128)S(1)}, u32[]{:S(2)}, u32[]{:S(2)}) collective-permute-start(f32[128,1024]{1,0:T(8,128)S(1)} %get-tuple-element.17.refs_0_), channel_id=1, source_target_pairs={{0,2},{2,4},{3,1},{4,6},{5,3},{6,8},{7,5},{8,10},{9,7},{10,12},{11... | collective-permute-start | bytes 1572872 | tf_op jit(solution)/shard_map/ppermute | solution.py:343
  42.1 15.5 %collective-permute-start.14 = (f32[32,256]{1,0:T(8,128)S(1)}, f32[32,256]{1,0:T(8,128)S(1)}, u32[]{:S(2)}, u32[]{:S(2)}) collective-permute-start(f32[32,256]{1,0:T(8,128)S(1)} %get-tuple-element.24), channel_id=1, source_target_pairs={{0,16},{1,17},{2,18},{3,19},{4,20},{5,21},{6,22},{7,23},{8,24},{9,... | collective-permute-start | bytes 98312 | tf_op jit(solution)/shard_map/ppermute | solution.py:338
  42.2 15.4 %collective-permute-start.15 = (f32[32,256]{1,0:T(8,128)S(1)}, f32[32,256]{1,0:T(8,128)S(1)}, u32[]{:S(2)}, u32[]{:S(2)}) collective-permute-start(f32[32,256]{1,0:T(8,128)S(1)} %get-tuple-element.24), channel_id=1, source_target_pairs={{0,24},{1,25},{2,26},{3,27},{4,28},{5,29},{6,30},{7,31},{8,16},{9,... | collective-permute-start | bytes 98312 | tf_op jit(solution)/shard_map/ppermute | solution.py:338
  47.3 7.4 %collective-permute-start.11 = (f32[32,1280]{1,0:T(8,128)S(1)}, f32[32,1280]{1,0:T(8,128)S(1)}, u32[]{:S(2)}, u32[]{:S(2)}) collective-permute-start(f32[32,1280]{1,0:T(8,128)S(1)} %get-tuple-element.23.middle.kept), channel_id=1, source_target_pairs={{0,1},{1,0},{2,3},{3,2},{4,5},{5,4},{6,7},{7,6},{8,9},{9,8},{10,11... | collective-permute-start | bytes 491528 | tf_op jit(solution)/shard_map/ppermute | solution.py:338
  47.3 7.4 %copy-start.6 = (s32[1,4,2]{1,2,0:T(2,128)S(1)}, s32[1,4,2]{1,2,0:T(2,128)}, u32[]{:S(2)}) copy-start(s32[1,4,2]{1,2,0:T(2,128)} %param.16) | copy-start | bytes 100
  47.3 7.4 %copy-start.8 = (f32[32]{0:T(128)S(1)}, f32[32]{0:T(128)}, u32[]{:S(2)}) copy-start(f32[32]{0:T(128)} %param.17) | copy-start | bytes 388
  47.3 10.6 %collective-permute-start.13 = (f32[32,768]{1,0:T(8,128)S(1)}, f32[32,768]{1,0:T(8,128)S(1)}, u32[]{:S(2)}, u32[]{:S(2)}) collective-permute-start(f32[32,768]{1,0:T(8,128)S(1)} %get-tuple-element.21.token), channel_id=1, source_target_pairs={{0,8},{1,9},{2,10},{3,11},{4,12},{5,13},{6,14},{7,15},{8,0},{9,1},... | collective-permute-start | bytes 294920 | tf_op jit(solution)/shard_map/ppermute | solution.py:338
  58.0 1.6 %collective-permute-start.16 = (f32[64,1024]{1,0:T(8,128)S(1)}, f32[64,1024]{1,0:T(8,128)S(1)}, u32[]{:S(2)}, u32[]{:S(2)}) collective-permute-start(f32[64,1024]{1,0:T(8,128)S(1)} %shard_map.106), channel_id=1, source_target_pairs={{0,1},{1,0},{2,3},{3,2},{4,5},{5,4},{6,7},{7,6},{8,9},{9,8},{10,11... | collective-permute-start | bytes 786440 | tf_op jit(solution)/shard_map/ppermute | solution.py:338
  58.1 3.3 %collective-permute-start.17 = (f32[32,1280]{1,0:T(8,128)S(1)}, f32[32,1280]{1,0:T(8,128)S(1)}, u32[]{:S(2)}, u32[]{:S(2)}) collective-permute-start(f32[32,1280]{1,0:T(8,128)S(1)} %shard_map.105.token.last), channel_id=1, source_target_pairs={{0,1},{1,0},{2,3},{3,2},{4,5},{5,4},{6,7},{7,6},{8,9},{9,8},{10,11... | collective-permute-start | bytes 491528 | tf_op jit(solution)/shard_map/ppermute | solution.py:338
